TPU v7x, 256 devices: a whole 4x4x8 slice. The times are simulated.
256 devices in a mesh: member: 4 (over z_lo), spec: 64 (over z_hi, y, x, core).
Axes of the slice: x: 4, y: 4, z: 8 (z_hi: 2, z_lo: 4; z = z_hi * 4 + z_lo), core: 2. Of those that a mesh axis runs over, the one named last changes fastest.
Arguments:
- spectra: bfloat16 [8, 1280, 2, 8, 1280], P('member', 'spec'), may hold values from -0.16992188 to 0.16992188
- legendre: bfloat16 [1280, 1280, 256], P('spec'), may hold values from -0.15625 to 0.15625
- assignment: int32 [1280], replicated, may hold values from 0 to 1279, each once
- clone_counts: int32 [8], replicated, may hold values from 0 to 4, as said below
- destinations: int32 [8], replicated, may hold values from 0 to 7, each once
Outputs:
- grid: float32 [8, 8, 512, 2560], P('member', None, 'spec')
- clone_weights: float32 [8], P('member')
- cloned: bfloat16 [8, 1280, 2, 8, 1280], P('member', 'spec')
Inputs may be any that keep to these rules, and one draw needn't show every extreme that they name: clone_counts sum to 8; the largest is exactly 4.
All inputs are finite; a program needn't handle non-finite values.
Results may differ from a plain program's by a relative error of at most 0.0065.
Values may be sent and summed in bfloat16 or wider, within the bound.
No kernel may reach another device: no remote copies, remote signals or barrier semaphores. Data moves between devices by JAX's collectives and lax.ppermute only.
A program may use at most 128 MiB of HBM per device.

v0:
```python
import math

import jax
import jax.numpy as jnp
from jax import lax
from jax.sharding import PartitionSpec as P

NLON = 2560


def parents(clone_counts, destinations):
    member_ids = jnp.arange(clone_counts.shape[0], dtype=jnp.int32)
    slot_of = jnp.sum(
        jnp.where(destinations[None, :] == member_ids[:, None], member_ids[None, :], 0), axis=1
    )
    bounds = jnp.cumsum(clone_counts)
    return jnp.sum((bounds[None, :] <= slot_of[:, None]).astype(jnp.int32), axis=1)


def on_device(spectra, legendre, assignment, clone_counts, destinations):
    spec_idx = lax.axis_index("spec")
    mem_local = spectra.shape[0]
    wave_count = spectra.shape[1]
    fields = spectra.shape[3]
    degree_count = spectra.shape[4]
    half_lats = legendre.shape[2]
    total_waves = assignment.shape[0]
    wave_local = lax.dynamic_slice_in_dim(assignment, spec_idx * wave_count, wave_count)
    degree_ids = jnp.arange(degree_count, dtype=jnp.int32)
    in_triangle = degree_ids[None, :] < (total_waves - wave_local)[:, None]
    masked = jnp.where(in_triangle[None, :, None, None, :], spectra, jnp.zeros((), spectra.dtype))
    coef_pairs = masked.reshape(mem_local, wave_count, 2, fields, degree_count // 2, 2)
    legendre_rows = legendre.reshape(wave_count, degree_count // 2, 2, half_lats)
    parity_sums = jnp.einsum(
        "imcfkp,mkpl->plcifm", coef_pairs, legendre_rows, preferred_element_type=jnp.float32
    )
    north_rows = parity_sums[0] + parity_sums[1]
    south_rows = (parity_sums[0] - parity_sums[1])[::-1]
    joined = jnp.concatenate([north_rows, south_rows], axis=0)
    fourier = joined.reshape(2 * half_lats, 2, mem_local * fields, wave_count).astype(jnp.bfloat16)
    longitudes = jnp.arange(NLON, dtype=jnp.int32)
    phase_index = assignment[:, None] * longitudes[None, :] % NLON
    angles = phase_index.astype(jnp.float32) * (2.0 * math.pi / NLON)
    weight = jnp.where(assignment == 0, 1.0, 2.0).astype(jnp.float32)[:, None]
    lon_table = jnp.stack([weight * jnp.cos(angles), -weight * jnp.sin(angles)])
    table_upper = lon_table.astype(jnp.bfloat16)
    table_rest = (lon_table - table_upper.astype(jnp.float32)).astype(jnp.bfloat16)
    fourier_block = lax.all_to_all(fourier, "spec", split_axis=0, concat_axis=3, tiled=True)
    upper_part = jnp.einsum(
        "lcgr,crx->glx", fourier_block, table_upper, preferred_element_type=jnp.float32
    )
    rest_part = jnp.einsum(
        "lcgr,crx->glx", fourier_block, table_rest, preferred_element_type=jnp.float32
    )
    grid_flat = upper_part + rest_part
    lat_dev = grid_flat.shape[1]
    grid_local = grid_flat.reshape(mem_local, fields, lat_dev, NLON)
    total_lats = lat_dev * lax.axis_size("spec")
    box_width = NLON // 4
    row_index = spec_idx * lat_dev + jnp.arange(lat_dev, dtype=jnp.int32)
    row_weight = 0.5 + row_index.astype(jnp.float32) / (total_lats - 1)
    sector = jnp.sum(grid_local[:, 0, :, :box_width], axis=2)
    partial_value = jnp.sum(sector * row_weight[None, :], axis=1) / math.sqrt(
        total_lats * box_width
    )
    member_idx = lax.axis_index("member")
    member_count = lax.axis_size("member")
    total_members = member_count * mem_local
    score_sum = lax.psum(partial_value, "spec")
    boosts = jnp.exp(score_sum)
    boost_total = lax.psum(jnp.sum(boosts), "member")
    weights = boosts * total_members / boost_total
    parent_all = parents(clone_counts, destinations)
    my_parents = lax.dynamic_slice_in_dim(parent_all, member_idx * mem_local, mem_local)
    piece = lax.all_gather(masked, "member", axis=0, tiled=True)
    member_rows = jnp.arange(piece.shape[0], dtype=jnp.int32)
    is_parent = (my_parents[:, None] == member_rows[None, :])[:, :, None, None, None, None]
    chosen = jnp.where(is_parent, piece[None], jnp.zeros((), piece.dtype))
    cloned = jnp.sum(chosen, axis=1)
    return (grid_local, weights, cloned)


def solution(mesh):
    placed = (P("member", "spec", None, None, None), P("spec", None, None), P(), P(), P())
    return jax.shard_map(
        on_device,
        mesh=mesh,
        in_specs=placed,
        out_specs=(
            P("member", None, "spec", None),
            P("member"),
            P("member", "spec", None, None, None),
        ),
        check_vma=False,
    )
```

profile of v0, /device:TPU:0, one launch (start us, length us, event | category | flops | bytes accessed | tf_op | source)
XLA Modules:
  0.0 432.5 jit_solution(1421328282024407010)
XLA Ops:
  7.2 0.8 dynamic-slice_subtract_fusion
  8.1 2.8 broadcast_select_fusion
  10.9 10.1 %copy.33 = bf16[2,20,2,8,1280]{1,3,4,2,0:T(8,128)(2,1)} copy(bf16[2,20,2,8,1280]{4,3,2,1,0:T(8,128)(2,1)} %broadcast_select_fusion) | data formatting | bytes 3276800 | tf_op jit(solution)/shard_map/jit(_where)/select_n | solution.py:31
  21.0 10.6 %copy.34 = bf16[2,20,2,8,640,2]{4,3,2,0,1,5:T(8,128)(2,1)S(1)} copy(bf16[2,20,2,8,640,2]{1,3,5,4,2,0:T(8,128)(2,1)} %bitcast.49) | data formatting | bytes 3276800 | tf_op jit(solution)/shard_map/reshape | solution.py:32
  31.7 19.9 %reshape.215 = bf16[20,640,2,256]{3,2,1,0:T(2,128)(2,1)} reshape(bf16[20,1280,256]{2,1,0:T(8,128)(2,1)} %param.6) | data formatting | bytes 26214400 | tf_op jit(solution)/shard_map/reshape | solution.py:33
  51.6 7.0 %fusion.26 = f32[2,256,2,2,8,20]{1,4,2,3,5,0:T(8,128)S(1)} fusion(bf16[2,20,2,8,640,2]{4,3,2,0,1,5:T(8,128)(2,1)S(1)} %copy.34, bf16[20,640,2,256,1,1]{3,2,1,0,5,4:T(2,128)(2,1)} %bitcast.48), kind=kOutput, calls=%fused_computation.24 | convolution fusion | flops 419430400 | bytes 16056320 | tf_op jit(solution)/shard_map/imcfkp,mkpl->plcifm/dot_general | solution.py:34
  58.8 0.4 rev.3
  59.3 7.0 %copy.37 = bf16[512,2,16,20]{3,2,1,0:T(8,128)(2,1)} copy(bf16[512,2,16,20]{0,2,3,1:T(8,128)(2,1)S(1)} %copy_bitcast_fusion) | data formatting | bytes 1310720 | tf_op jit(solution)/shard_map/convert_element_type | solution.py:40
  66.3 10.5 %reshape.224 = bf16[64,2,2560]{2,1,0:T(2,128)(2,1)} reshape(bf16[512,2,16,20]{3,2,1,0:T(8,128)(2,1)} %copy.37) | data formatting | bytes 1310720
  76.8 13.0 %all-to-all-start = ((bf16[64,2,2560]{2,1,0:T(2,128)(2,1)}), bf16[64,2,2560]{2,1,0:T(2,128)(2,1)S(1)}, u32[]{:S(2)}, u32[]{:S(2)}) async-start(bf16[64,2,2560]{2,1,0:T(2,128)(2,1)} %reshape.224), calls=%async_computation | async-start | bytes 1310720 | tf_op jit(solution)/shard_map/all_to_all | solution.py:48
  89.9 57.7 %cosine_multiply_fusion = (f32[1,1280,2560]{2,1,0:T(8,128)}, f32[1,1280,2560]{2,1,0:T(8,128)}) fusion(s32[1280]{0:T(1024)S(1)} %copy-done, f32[1280]{0:T(1024)S(1)} %get-tuple-element.20, f32[1280]{0:T(1024)S(1)} %get-tuple-element.21), kind=kLoop, calls=%fused_computation.12 | loop fusion | flops 36044800 | bytes 26229760 | tf_op jit(solution)/shard_map/mul | solution.py:45
  148.0 11.3 %reshape.225 = bf16[512,2,16,20]{3,2,1,0:T(8,128)(2,1)} reshape(bf16[64,2,2560]{2,1,0:T(2,128)(2,1)S(1)} %all-to-all-done) | data formatting | bytes 1310720
  159.4 6.8 %copy.38 = bf16[8,2,16,64,20]{4,3,2,1,0:T(8,128)(2,1)} copy(bf16[8,2,16,64,20]{4,2,1,0,3:T(8,128)(2,1)} %bitcast.50) | data formatting | bytes 1310720 | tf_op jit(solution)/shard_map/all_to_all | solution.py:48
  166.2 8.1 %all_to_all.16 = bf16[8,2,16,1280]{3,2,1,0:T(8,128)(2,1)S(1)} reshape(bf16[8,2,16,64,20]{4,3,2,1,0:T(8,128)(2,1)} %copy.38) | data formatting | bytes 1310720 | tf_op jit(solution)/shard_map/all_to_all | solution.py:48
  174.3 9.7 %fusion.23 = f32[2560,8,16]{0,2,1:T(8,128)S(1)} fusion(bf16[8,2,16,1280]{3,2,1,0:T(8,128)(2,1)S(1)} %all_to_all.16, f32[1,1280,2560]{2,1,0:T(8,128)} %get-tuple-element.19, f32[1,1280,2560]{2,1,0:T(8,128)} %get-tuple-element.18), kind=kOutput, calls=%fused_computation.22 | convolution fusion | flops 1710489600 | bytes 28180480 | tf_op jit(solution)/shard_map/lcgr,crx->glx/dot_general | solution.py:52
  184.0 1.2 slice-done.2
  185.2 1.2 slice-done.3
  186.4 6.3 %fusion.20 = f32[2,8,8,2560]{3,1,0,2:T(8,128)S(1)} fusion(f32[2560,8,16]{0,2,1:T(8,128)S(1)} %fusion.23, bf16[8,2,16,1280]{3,2,1,0:T(8,128)(2,1)S(1)} %all_to_all.16, f32[1,1280,2560]{2,1,0:T(8,128)} %get-tuple-element.19, f32[1,1280,2560]{2,1,0:T(8,128)S(1)} %bitcast.52), kind=kOutput, calls=%fused_computation.21 | convolution fusion | flops 1704263680 | bytes 29491200 | tf_op jit(solution)/shard_map/lcgr,crx->glx/dot_general | solution.py:49
  193.0 210.5 %psum.14 = f32[2]{0:T(128)S(1)} all-reduce(f32[2]{0:T(128)S(1)} %broadcast_multiply_fusion), channel_id=1, replica_groups=mesh['member'=4,'spec'=64] {'spec'}, use_global_device_ids=true, to_apply=%region_2.3 | all-reduce | flops 2 | bytes 16 | tf_op jit(solution)/shard_map/psum | solution.py:69
  403.5 0.6 exponential_reduce_fusion
  404.2 11.2 %psum.15 = f32[]{:T(128)} all-reduce(f32[]{:T(128)} %exponential_reduce_fusion), channel_id=1, replica_groups=mesh['member'=4,'spec'=64] {'member'}, use_global_device_ids=true, to_apply=%region_4.5 | all-reduce | flops 1 | bytes 8 | tf_op jit(solution)/shard_map/psum | solution.py:71
  415.4 1.8 copy.39
  417.2 1.2 multiply_divide_fusion
  418.4 7.2 %select_reduce_fusion = bf16[2,20,2,8,1280]{4,3,2,1,0:T(8,128)(2,1)} fusion(pred[2,8]{1,0:T(4,128)(4,1)S(1)} %iota_compare_fusion.2, bf16[8,20,2,8,1280]{4,3,2,1,0:T(8,128)(2,1)} %all-gather.2.cloned.1.call-done), kind=kLoop, calls=%fused_computation.10 | loop fusion | flops 12288000 | bytes 8192016 | tf_op jit(solution)/shard_map/reduce_sum | solution.py:79
  (31 shorter events, 1.3 us)
Async XLA Ops:
  7.2 411.2 %all-gather.2.cloned.1.call-start = ((), (), s32[]{:S(2)}) async-start(), calls=%async_computation.1 | async-start | bytes 8192000 | tf_op jit(solution)/shard_map/all_gather | solution.py:75
  58.6 31.3 %copy-start = (s32[1280]{0:T(1024)S(1)}, s32[1280]{0:T(1024)}, u32[]{:S(2)}) copy-start(s32[1280]{0:T(1024)} %param.7) | copy-start | bytes 15364
  76.8 71.2 %all-to-all-start = ((bf16[64,2,2560]{2,1,0:T(2,128)(2,1)}), bf16[64,2,2560]{2,1,0:T(2,128)(2,1)S(1)}, u32[]{:S(2)}, u32[]{:S(2)}) async-start(bf16[64,2,2560]{2,1,0:T(2,128)(2,1)} %reshape.224), calls=%async_computation | async-start | bytes 1310720 | tf_op jit(solution)/shard_map/all_to_all | solution.py:48
  89.9 57.7 %copy-start.1 = (s32[8]{0:T(128)S(1)}, s32[8]{0:T(128)}, u32[]{:S(2)}) copy-start(s32[8]{0:T(128)} %param.8) | copy-start | bytes 100
  89.9 57.9 %copy-start.2 = (s32[8]{0:T(128)S(1)}, s32[8]{0:T(128)}, u32[]{:S(2)}) copy-start(s32[8]{0:T(128)} %param.9) | copy-start | bytes 100
  166.2 17.8 %slice-start = ((s8[13107200]{0:T(1024)(128)(4,1)}), s8[524288]{0:T(1024)(128)(4,1)S(1)}, s32[]{:S(2)}) async-start(s8[13107200]{0:T(1024)(128)(4,1)} %bitcast.51), calls=%async_computation.2 | async-start | bytes 1048576
  174.3 9.7 %slice-start.1 = ((s8[13107200]{0:T(1024)(128)(4,1)}), s8[4194304]{0:T(1024)(128)(4,1)S(1)}, s32[]{:S(2)}) async-start(s8[13107200]{0:T(1024)(128)(4,1)} %bitcast.51), calls=%async_computation.3 | async-start | bytes 8388608
  174.3 10.9 %slice-start.2 = ((s8[13107200]{0:T(1024)(128)(4,1)}), s8[4194304]{0:T(1024)(128)(4,1)S(1)}, s32[]{:S(2)}) async-start(s8[13107200]{0:T(1024)(128)(4,1)} %bitcast.51), calls=%async_computation.4 | async-start | bytes 8388608
  174.3 12.1 %slice-start.3 = ((s8[13107200]{0:T(1024)(128)(4,1)}), s8[4194304]{0:T(1024)(128)(4,1)S(1)}, s32[]{:S(2)}) async-start(s8[13107200]{0:T(1024)(128)(4,1)} %bitcast.51), calls=%async_computation.5 | async-start | bytes 8388608
Sparse Core Ops, SparseCore 0:
  11.0 138.1 all-gather.1
where the time goes:
time: 434 us; the launch traced here: 432 us
  blocking collectives  222 us (51%)
  local copies, waits for them, and re-layouts  89.1 us (21%)
  other arithmetic  71.5 us (16%)
  matrix products  23 us (5%)
  between operations  14.2 us (3%)
  starting transfers between devices  13 us (3%)
    psum x1, blocking collectives, on_device(): score_sum = lax.psum(partial_value, 'spec')  211 us
    mul x1, other arithmetic, on_device(): lon_table = jnp.stack([weight * jnp.cos(angles), -weight * jnp.sin(angles)])  57.7 us
    unnamed x17, local copies, waits for them, and re-layouts  26.1 us
    reshape x1, local copies, waits for them, and re-layouts, on_device(): legendre.reshape(wave_count, degree_count // 2, 2, half_lats)  19.9 us
    all_to_all x2, local copies, waits for them, and re-layouts, on_device(): lax.all_to_all(fourier, 'spec', split_axis=0, concat_axis=3, tiled=True)  14.9 us
    all_to_all x1, starting transfers between devices, on_device(): lax.all_to_all(fourier, 'spec', split_axis=0, concat_axis=3, tiled=True)  13 us
    psum x1, blocking collectives, on_device(): boost_total = lax.psum(jnp.sum(boosts), 'member')  11.2 us
    reshape x1, local copies, waits for them, and re-layouts, on_device(): masked.reshape(mem_local, wave_count, 2, fields, degree_count // 2, 2)  10.6 us
  transfers between devices with their start and end apart: 2, of which 0 were waited for; matrix products, arithmetic and copies ran while one was open for 37% of the time, Pallas kernels for 0%

commit v1 on v0

v1 whole, which is shorter than its diff:
```python
import math

import jax
import jax.numpy as jnp
from jax import lax
from jax.experimental import pallas as pl
from jax.experimental.pallas import tpu as pltpu
from jax.sharding import PartitionSpec as P

NLON = 2560
NN = 1280
HALF = NLON // 2
TILES = HALF // 256
ROWS = 20
SPEC = 64
MEM = 4
GROUP = 4
STEPS = ROWS // GROUP
KEEP = 2 * ROWS
SENT = KEEP + 8
DEPTH = SPEC * KEEP
CHUNKS = NN // 128
CAP = 152
ROUNDS = 3
SLOT = 6
FINE = 8
OFF = 16
LEN = 36
RIGHT = [(0, 1), (1, 2), (2, 3)]
LEFT = [(1, 0), (2, 1), (3, 2)]
COSINE = [(-1) ** k * math.pi ** (2 * k) / math.factorial(2 * k) for k in range(10)]
ANY = pl.BlockSpec(memory_space=pl.ANY)
SMEM = pl.BlockSpec(memory_space=pltpu.SMEM)
VMEM = pl.BlockSpec(memory_space=pltpu.VMEM)
PARAMS = pltpu.CompilerParams(vmem_limit_bytes=16 * 1024 * 1024)
LARGE = pltpu.CompilerParams(vmem_limit_bytes=56 * 1024 * 1024)


def pick(mask, codes):
    total = jnp.int32(0)
    for p, code in enumerate(codes):
        if code is not None:
            total = total + jnp.where((mask >> p) & 1 == 1, code, 0)
    return total


def plan(counts, dest, par, table):
    bounds = []
    total = jnp.int32(0)
    for s in range(8):
        total = total + counts[s]
        bounds.append(total)
    for k in range(8):
        parent = jnp.int32(0)
        for s in range(8):
            parent = parent + jnp.where(bounds[s] <= k, 1, 0)
        par[dest[k]] = parent
    one = jnp.int32(1)
    need = [(one << par[2 * d]) | (one << par[2 * d + 1]) for d in range(MEM)]
    have = [jnp.int32(3 << (2 * c)) for c in range(MEM)]
    code = [[jnp.int32(p % 2) if p // 2 == c else jnp.int32(0) for p in range(8)] for c in range(MEM)]
    for t in range(ROUNDS):
        moves = []
        for c in range(MEM - 1):
            west = (1 << (2 * (c + 1))) - 1
            for way, a, b, homes, order in (
                (0, c, c + 1, west, range(MEM - 1, c, -1)),
                (1, c + 1, c, 255 - west, range(0, c + 1)),
            ):
                open_mask = have[a] & ~have[b] & homes
                chosen = jnp.int32(0)
                for d in reversed(list(order)):
                    wanted = open_mask & need[d]
                    chosen = jnp.where(wanted != 0, wanted, chosen)
                chosen = chosen & -chosen
                moves.append((way, a, b, chosen))
        for way, a, b, chosen in moves:
            table[a, 2 * t + way] = pick(chosen, code[a])
        for way, a, b, chosen in moves:
            have[b] = have[b] | chosen
            for p in range(8):
                code[b][p] = jnp.where((chosen >> p) & 1 == 1, 2 + 2 * t + way, code[b][p])
    fine = jnp.int32(1)
    for d in range(MEM):
        fine = jnp.where(need[d] & ~have[d] == 0, fine, 0)
        for s in range(2):
            table[d, SLOT + s] = pick(one << par[2 * d + s], code[d])
    return fine


def pack_kernel(counts, dest, assignment, place, spectra, tab, own, right, left, held, packed, par, table, sems):
    fetch = pltpu.make_async_copy(spectra, held, sems.at[0])
    fetch.start()
    for c in range(MEM):
        for i in range(2 * ROUNDS):
            table[c, i] = 0
    fine = plan(counts, dest, par, table)
    for i in range(2 * ROUNDS + 2):
        tab[i] = table[place[0], i]
    tab[FINE] = fine
    total = jnp.int32(0)
    for r in range(ROWS):
        length = NN - assignment[place[1] * ROWS + r]
        tab[OFF + r] = jnp.minimum(total, CAP)
        tab[LEN + r] = length
        total = total + ((length + 127) >> 7)
    fetch.wait()

    def row(r, carry):
        start = tab[OFF + r]
        for m in range(2):
            for k in range(CHUNKS):
                packed[m, start + k] = held[m, r, :, k * 128 : (k + 1) * 128]
        return carry

    lax.fori_loop(0, ROWS, row, 0)
    copies = [
        pltpu.make_async_copy(packed.at[tab[0], pl.ds(0, CAP)], right, sems.at[1]),
        pltpu.make_async_copy(packed.at[tab[1], pl.ds(0, CAP)], left, sems.at[2]),
        pltpu.make_async_copy(packed.at[0, pl.ds(0, CAP)], own.at[0], sems.at[3]),
        pltpu.make_async_copy(packed.at[1, pl.ds(0, CAP)], own.at[1], sems.at[4]),
    ]
    for copy in copies:
        copy.start()
    for copy in copies:
        copy.wait()


def pack(counts, dest, assignment, place, spectra):
    slab = jax.ShapeDtypeStruct((CAP, 16, 128), jnp.bfloat16)
    return pl.pallas_call(
        pack_kernel,
        name="pack",
        in_specs=[SMEM, SMEM, SMEM, SMEM, ANY],
        out_specs=[SMEM, ANY, ANY, ANY],
        out_shape=[
            jax.ShapeDtypeStruct((64,), jnp.int32),
            jax.ShapeDtypeStruct((2, CAP, 16, 128), jnp.bfloat16),
            slab,
            slab,
        ],
        scratch_shapes=[
            pltpu.VMEM((2, ROWS, 16, NN), jnp.bfloat16),
            pltpu.VMEM((2, CAP + 16, 16, 128), jnp.bfloat16),
            pltpu.SMEM((8,), jnp.int32),
            pltpu.SMEM((MEM, 8), jnp.int32),
            pltpu.SemaphoreType.DMA((5,)),
        ],
        compiler_params=PARAMS,
        cost_estimate=pl.CostEstimate(flops=0, bytes_accessed=6_000_000, transcendentals=0),
    )(counts, dest, assignment, place, spectra)


def choose(code, slabs, target, sem):
    for k, slab in enumerate(slabs):

        @pl.when(code == k)
        def _():
            pltpu.make_async_copy(slab, target, sem).start()


def relay(t, way, tab, own, arrived, after):
    def kernel(*refs):
        tab_ref, own_ref = refs[0], refs[1]
        slabs = [own_ref.at[0], own_ref.at[1], *refs[2 : 2 + t]]
        out, sem = refs[-2], refs[-1]
        code = tab_ref[2 * t + way]
        for k, slab in enumerate(slabs):

            @pl.when(code == (k if k < 2 else 2 + 2 * (k - 2) + way))
            def _():
                pltpu.make_async_copy(slab, out, sem).start()

        pltpu.make_async_copy(slabs[0], out, sem).wait()

    return pl.pallas_call(
        kernel,
        name="relay%d%s" % (t, "rl"[way]),
        in_specs=[SMEM] + [ANY] * (2 + t),
        out_specs=ANY,
        out_shape=jax.ShapeDtypeStruct((CAP, 16, 128), jnp.bfloat16),
        scratch_shapes=[pltpu.SemaphoreType.DMA],
        compiler_params=PARAMS,
        cost_estimate=pl.CostEstimate(flops=0, bytes_accessed=1_300_000, transcendentals=0),
    )(tab, own, *arrived, after)


def hold_kernel(*refs):
    pass


def hold(value, *after):
    return pl.pallas_call(
        hold_kernel,
        name="hold",
        in_specs=[ANY] * (1 + len(after)),
        out_specs=ANY,
        out_shape=jax.ShapeDtypeStruct(value.shape, value.dtype),
        input_output_aliases={0: 0},
        compiler_params=PARAMS,
        cost_estimate=pl.CostEstimate(flops=30_000_000_000, bytes_accessed=0, transcendentals=0),
    )(value, *after)


def unpack_kernel(*refs):
    tab, own, *rest = refs
    slabs = [own.at[0], own.at[1], *rest[: 2 * ROUNDS]]
    out, plain, packed, sems = rest[2 * ROUNDS + 1 :]
    for s in range(2):
        choose(tab[SLOT + s], slabs, packed.at[s, pl.ds(0, CAP)], sems.at[s])
    for s in range(2):
        pltpu.make_async_copy(own.at[0], packed.at[s, pl.ds(0, CAP)], sems.at[s]).wait()
        lane = lax.broadcasted_iota(jnp.int32, (16, 128), 1)

        def row(r, carry):
            start = tab[OFF + r]
            length = tab[LEN + r]
            for k in range(CHUNKS):
                value = packed[s, start + k]
                kept = jnp.where(lane + k * 128 < length, value, jnp.zeros_like(value))
                plain[s, r, :, k * 128 : (k + 1) * 128] = kept
            return carry

        lax.fori_loop(0, ROWS, row, 0)
        pltpu.make_async_copy(plain.at[s], out.at[s], sems.at[2 + s]).start()
    for s in range(2):
        pltpu.make_async_copy(plain.at[s], out.at[s], sems.at[2 + s]).wait()


def unpack(tab, own, arrived, after):
    return pl.pallas_call(
        unpack_kernel,
        name="unpack",
        in_specs=[SMEM] + [ANY] * (2 + 2 * ROUNDS),
        out_specs=ANY,
        out_shape=pltpu.HBM((2, ROWS, 16, NN), jnp.bfloat16),
        scratch_shapes=[
            pltpu.VMEM((2, ROWS, 16, NN), jnp.bfloat16),
            pltpu.VMEM((2, CAP + 16, 16, 128), jnp.bfloat16),
            pltpu.SemaphoreType.DMA((4,)),
        ],
        compiler_params=PARAMS,
        cost_estimate=pl.CostEstimate(flops=0, bytes_accessed=3_000_000, transcendentals=0),
    )(tab, own, *arrived, after)


def swap_blocks(x):
    t = lax.broadcasted_iota(jnp.int32, x.shape, 1)
    s = lax.broadcasted_iota(jnp.int32, x.shape, 2) >> 4
    for k in (1, 2, 4):
        low_t = (t & k) == 0
        low_s = (s & k) == 0
        up = pltpu.roll(pltpu.roll(x, 8 - k, 1), 16 * k, 2)
        down = up if k == 4 else pltpu.roll(pltpu.roll(x, k, 1), 128 - 16 * k, 2)
        x = jnp.where(low_t == low_s, x, jnp.where(low_t, up, down))
    return x


def cosine(phase):
    phase = phase - NLON * jnp.floor(phase * (1.0 / NLON) + 0.5)
    part = phase * (2.0 / NLON)
    square = part * part
    total = COSINE[-1]
    for factor in COSINE[-2::-1]:
        total = total * square + factor
    return total


def sector(wave):
    a = jnp.full((8, 128), wave, jnp.int32).astype(jnp.float32)
    x = lax.broadcasted_iota(jnp.int32, (8, 128), 0) * 128 + lax.broadcasted_iota(jnp.int32, (8, 128), 1)
    phase = a * x.astype(jnp.float32)
    weight = jnp.where(a == 0.0, 1.0, 2.0) * (1.0 / math.sqrt(512 * (NLON // 4)))
    weight = jnp.where(x < NLON // 4, weight, 0.0)
    return [
        jnp.sum(jnp.sum(v * weight, axis=0, keepdims=True), axis=1, keepdims=True) for v in (cosine(phase), cosine(phase + NLON // 4))
    ]


def legendre_kernel(tab, spectra, legendre, out, blocks, sums):
    q = pl.program_id(0)
    lats = lax.broadcasted_iota(jnp.int32, (1, 256), 1).astype(jnp.float32)
    north = 0.5 + lats * (1.0 / 511.0)
    south = 0.5 + (511.0 - lats) * (1.0 / 511.0)

    @pl.when(q == 0)
    def _():
        sums[...] = jnp.zeros_like(sums)

    lane = lax.broadcasted_iota(jnp.int32, (32, NN), 1)
    odd = (lane & 1) == 1
    sides = [[None] * 16, [None] * 16]
    totals = [sums[0:1, :], sums[1:2, :]]
    for r in range(GROUP):
        length = tab[LEN + q * GROUP + r]
        factors = sector(NN - length)
        x = spectra[:, r].reshape(32, NN)
        x = jnp.where(lane < length, x, jnp.zeros_like(x))
        signed = jnp.where(odd, -x, x)
        both = jnp.concatenate([x, signed], axis=0)
        got = jnp.dot(both, legendre[r], preferred_element_type=jnp.float32)
        for c in range(2):
            for i in range(2):
                at = i * 16 + c * 8
                for side in range(2):
                    sides[side][(c * GROUP + r) * 2 + i] = got[side * 32 + at : side * 32 + at + 8]
                up, down = (
                    got[k : k + 1].astype(jnp.bfloat16).astype(jnp.float32) for k in (at, 32 + at)
                )
                totals[i] = totals[i] + factors[c] * (up * north + down * south)
    sums[0:1, :] = totals[0]
    sums[1:2, :] = totals[1]
    rows = pl.ds(pl.multiple_of(q * 8, 8), 8)
    upper = swap_blocks(jnp.concatenate(sides[0], axis=0).T.reshape(32, 8, 128))
    blocks[0:32, rows, :] = upper
    lower = swap_blocks(jnp.concatenate(sides[1], axis=0).T.reshape(32, 8, 128))
    for b in range(32):
        blocks[63 - b, rows, :] = lower[b]

    @pl.when(q == STEPS - 1)
    def _():
        at = lax.broadcasted_iota(jnp.int32, (8, 128), 0)
        parts = jnp.zeros((8, 128), jnp.float32)
        for i in range(2):
            left = jnp.sum(totals[i], axis=1, keepdims=True)
            for k in range(3):
                part = left.astype(jnp.bfloat16).astype(jnp.float32)
                left = left - part
                parts = jnp.where(at == 2 * k + i, part, parts)
        blocks[:, KEEP:SENT, :] = jnp.broadcast_to(parts[None], (SPEC, 8, 128))
        out[...] = blocks[...].astype(jnp.bfloat16)


def legendre_sums(tab, spectra, legendre):
    return pl.pallas_call(
        legendre_kernel,
        name="legendre",
        grid=(STEPS,),
        in_specs=[
            SMEM,
            pl.BlockSpec((2, GROUP, 16, NN), lambda q: (0, q, 0, 0)),
            pl.BlockSpec((GROUP, NN, 256), lambda q: (q, 0, 0)),
        ],
        out_specs=pl.BlockSpec((SPEC, SENT, 128), lambda q: (0, 0, 0)),
        out_shape=jax.ShapeDtypeStruct((SPEC, SENT, 128), jnp.bfloat16),
        scratch_shapes=[
            pltpu.VMEM((SPEC, SENT, 128), jnp.float32),
            pltpu.VMEM((2, 256), jnp.float32),
        ],
        compiler_params=LARGE,
        cost_estimate=pl.CostEstimate(flops=900_000_000, bytes_accessed=16_000_000, transcendentals=0),
    )(tab, spectra, legendre)


def table_kernel(tab, waves, after, out, sign, fast, counted, held, sems):
    step = pl.program_id(0)
    slot = step & 1
    own = waves[pl.ds(step, 1), :]
    high = jnp.floor(own * (1.0 / 64))
    k = lax.broadcasted_iota(jnp.int32, (256, 128), 0)
    n = lax.broadcasted_iota(jnp.int32, (256, 128), 1)
    spread = ((k >> 3) * 4 + (k & 3) == n).astype(jnp.float32).astype(jnp.bfloat16)

    def column(row):
        rows = jnp.broadcast_to(row, (128, 128)).astype(jnp.bfloat16)
        return lax.dot_general(spread, rows, (((1,), (1,)), ((), ())), preferred_element_type=jnp.float32)

    a = 64.0 * column(high) + column(own - 64.0 * high)
    parity = own - 2.0 * jnp.floor(own * 0.5)
    signs = jnp.broadcast_to(1.0 - 2.0 * parity, (8, 128)).astype(jnp.bfloat16)
    sign[...] = lax.dot_general(signs, spread, (((1,), (1,)), ((), ())), preferred_element_type=jnp.float32)

    @pl.when(step == 0)
    def _():
        counted[...] = jnp.zeros_like(counted)

    chunks = jnp.floor((NN + 127.0 - own) * (1.0 / 128))
    place = lax.broadcasted_iota(jnp.int32, (128, 128), 0) + step * 128
    first = lax.broadcasted_iota(jnp.int32, (128, 128), 1) * ROWS
    within = ((place >= first) & (place < first + ROWS)).astype(jnp.float32).astype(jnp.bfloat16)
    counted[...] += jnp.dot(
        jnp.broadcast_to(chunks, (8, 128)).astype(jnp.bfloat16), within, preferred_element_type=jnp.float32
    )

    def store(at):
        rows = pl.ds(pl.multiple_of(at * 256, 256), 256)
        return pltpu.make_async_copy(held.at[at & 1], out.at[:, rows, :], sems.at[at & 1])

    @pl.when(step >= 2)
    def _():
        store(step - 2).wait()

    piece = 64
    lane = n[:piece].astype(jnp.float32)
    part = ((k[:piece] >> 2) & 1).astype(jnp.float32) * (NLON // 4)
    for i in range(0, 256, piece):
        wave = a[i : i + piece]
        weight = jnp.where(wave == 0.0, 1.0, 2.0)
        turn = wave * 128.0
        phase = wave * lane + part
        now = cosine(phase) * weight
        later = cosine(phase + turn) * weight
        twice = 2.0 * cosine(turn)
        for j in range(HALF // 128):
            at = (j % 2) * 128
            held[slot, j // 2, i : i + piece, at : at + 128] = now.astype(jnp.bfloat16)
            now, later = later, twice * later - now

    store(step).start()

    @pl.when(step == DEPTH // 256 - 1)
    def _():
        most = jnp.max(counted[...]).astype(jnp.int32)
        fast[0] = jnp.where((most <= CAP) & (tab[FINE] == 1), 1, 0)
        store(step - 1).wait()
        store(step).wait()


def make_table(tab, waves, after):
    block = 256
    return pl.pallas_call(
        table_kernel,
        name="table",
        grid=(DEPTH // block,),
        in_specs=[SMEM, pl.BlockSpec((10, 128), lambda i: (0, 0)), ANY],
        out_specs=[
            ANY,
            pl.BlockSpec((8, block), lambda i: (0, i)),
            SMEM,
        ],
        out_shape=[
            pltpu.HBM((TILES, DEPTH, 256), jnp.bfloat16),
            jax.ShapeDtypeStruct((8, DEPTH), jnp.float32),
            jax.ShapeDtypeStruct((1,), jnp.int32),
        ],
        scratch_shapes=[
            pltpu.VMEM((8, 128), jnp.float32),
            pltpu.VMEM((2, TILES, block, 256), jnp.bfloat16),
            pltpu.SemaphoreType.DMA((2,)),
        ],
        compiler_params=PARAMS,
        cost_estimate=pl.CostEstimate(flops=60_000_000_000, bytes_accessed=8_000_000, transcendentals=0),
    )(tab, waves, after)


def grid_kernel(south, blocks, sign, table, out, boosts, arrived, held, stacked, result, sems):
    first = pltpu.make_async_copy(blocks, arrived, sems.at[0])
    first.start()
    tiles = [pltpu.make_async_copy(table.at[j], held.at[j], sems.at[1 + j]) for j in range(TILES)]
    for tile in tiles:
        tile.start()
    first.wait()
    rows = arrived[...].astype(jnp.float32)[:, :KEEP, :].reshape(DEPTH, 128).astype(jnp.bfloat16)
    to = lax.broadcasted_iota(jnp.int32, (128, 128), 0)
    by = lax.broadcasted_iota(jnp.int32, (128, 128), 1)
    lat = jnp.where(south[0] == 1, 7 - (to & 7), to & 7)
    order = (by == lat * 16 + (to >> 3)).astype(jnp.float32).astype(jnp.bfloat16)
    turned = lax.dot_general(order, rows, (((1,), (1,)), ((), ())), preferred_element_type=jnp.float32)
    stacked[0:128, :] = turned.astype(jnp.bfloat16)
    stacked[128:256, :] = (turned * sign[0:1, :]).astype(jnp.bfloat16)
    parts = jnp.sum(arrived[:, KEEP:SENT, :].astype(jnp.float32), axis=0)
    values = jnp.exp(parts[0:2] + parts[2:4] + parts[4:6])
    boosts[...] = jnp.concatenate([values, values, values[0:1] + values[1:2], jnp.zeros((3, 128))], axis=0)
    stores = []
    for j in range(TILES):
        tiles[j].wait()
        got = jnp.dot(stacked[...], held[j], preferred_element_type=jnp.float32)
        for half in range(2):
            at = pl.ds(half * HALF + j * 256, 256)
            result[:, at] = got[half * 128 : half * 128 + 128]
            stores.append(pltpu.make_async_copy(result.at[:, at], out.at[:, at], sems.at[1 + TILES + 2 * j + half]))
            stores[-1].start()
    for store in stores:
        store.wait()


def make_grid(south, blocks, sign, table):
    return pl.pallas_call(
        grid_kernel,
        name="dft",
        in_specs=[SMEM, ANY, VMEM, ANY],
        out_specs=[ANY, VMEM],
        out_shape=[
            pltpu.HBM((128, NLON), jnp.float32),
            jax.ShapeDtypeStruct((8, 128), jnp.float32),
        ],
        scratch_shapes=[
            pltpu.VMEM((SPEC, SENT, 128), jnp.bfloat16),
            pltpu.VMEM((TILES, DEPTH, 256), jnp.bfloat16),
            pltpu.VMEM((256, DEPTH), jnp.bfloat16),
            pltpu.VMEM((128, NLON), jnp.float32),
            pltpu.SemaphoreType.DMA((1 + 3 * TILES,)),
        ],
        compiler_params=LARGE,
        cost_estimate=pl.CostEstimate(flops=60_000_000_000, bytes_accessed=9_000_000, transcendentals=0),
    )(south, blocks, sign, table)


def on_device(spectra, legendre, assignment, clone_counts, destinations):
    spec_idx = lax.axis_index("spec")
    member_idx = lax.axis_index("member")
    rows = spectra.reshape(2, ROWS, 16, NN)

    place = jnp.stack([member_idx, spec_idx]).astype(jnp.int32)
    tab, own, right, left = pack(clone_counts, destinations, assignment, place, rows)
    rights = [lax.ppermute(right, "member", RIGHT)]
    lefts = [lax.ppermute(left, "member", LEFT)]
    sent = legendre_sums(tab, rows, legendre)

    right = relay(1, 0, tab, own, rights, sent)
    rights.append(lax.ppermute(right, "member", RIGHT))
    left = relay(1, 1, tab, own, lefts, right)
    lefts.append(lax.ppermute(left, "member", LEFT))
    blocks = lax.all_to_all(hold(sent, right, left), "spec", split_axis=0, concat_axis=0, tiled=True)

    right = relay(2, 0, tab, own, rights, left)
    rights.append(lax.ppermute(right, "member", RIGHT))
    left = relay(2, 1, tab, own, lefts, right)
    lefts.append(lax.ppermute(left, "member", LEFT))
    arrived = [slab for pair in zip(rights, lefts) for slab in pair]

    table, sign, fast = make_table(tab, assignment.astype(jnp.float32).reshape(10, 128), left)
    south = (spec_idx >= SPEC // 2).astype(jnp.int32).reshape(1)
    flat, boosts = make_grid(south, blocks, sign, table)
    grid = flat.reshape(2, 8, 8, NLON)
    total = boosts
    for o in range(1, MEM):
        total = total + lax.ppermute(boosts, "member", [(s, (s + o) % MEM) for s in range(MEM)])
    weights = boosts[0:2, 0] * 8.0 / total[4, 0]

    def general():
        wave = lax.dynamic_slice_in_dim(assignment, spec_idx * ROWS, ROWS)
        inside = jnp.arange(NN, dtype=jnp.int32)[None, :] < (NN - wave)[:, None]
        masked = jnp.where(inside[None, :, None, :], rows, jnp.zeros((), rows.dtype))
        bounds = jnp.cumsum(clone_counts)
        ids = jnp.arange(8, dtype=jnp.int32)
        slot = jnp.sum(jnp.where(destinations[None, :] == ids[:, None], ids[None, :], 0), axis=1)
        parent = jnp.sum((bounds[None, :] <= slot[:, None]).astype(jnp.int32), axis=1)
        mine_now = lax.dynamic_slice_in_dim(parent, member_idx * 2, 2)
        cloned = jnp.zeros_like(rows)
        for o in range(MEM):
            block = masked
            if o > 0:
                block = lax.ppermute(masked, "member", [(s, (s + o) % MEM) for s in range(MEM)])
            home = (member_idx - o) % MEM
            for i in range(2):
                cloned = jnp.where((mine_now == home * 2 + i)[:, None, None, None], block[i][None], cloned)
        return cloned

    cloned = lax.cond(fast[0] == 1, lambda: unpack(tab, own, arrived, flat), general)
    return grid, weights, cloned.reshape(2, ROWS, 2, 8, NN)


def solution(mesh):
    placed = (P("member", "spec", None, None, None), P("spec", None, None), P(), P(), P())
    return jax.shard_map(
        on_device,
        mesh=mesh,
        in_specs=placed,
        out_specs=(
            P("member", None, "spec", None),
            P("member"),
            P("member", "spec", None, None, None),
        ),
        check_vma=False,
    )
```

time: 434 us -> 90.5 us (0.21)
  the two profiles are of different devices: /device:TPU:0 before, /device:TPU:24 now
where the time goes in v1:
time: 90.5 us; the launch traced here: 89.9 us
  Pallas kernels  38 us (42%)
  starting transfers between devices  37.3 us (41%)
  waiting for transfers between devices  10.6 us (12%)
  between operations  1.47 us (2%)
  other arithmetic  1.34 us (1%)
  local copies, waits for them, and re-layouts  1.27 us (1%)
    all_to_all x1, starting transfers between devices, on_device(): lax.all_to_all(hold(sent, right, left), 'spec', split_axis=0, concat_axis...  13.7 us
    ppermute x2, starting transfers between devices, on_device(): rights.append(lax.ppermute(right, 'member', RIGHT))  10.7 us
    pallas_call x1, Pallas kernels, make_table(): pl.pallas_call(table_kernel, name='table', grid=(DEPTH // block,), in_spe...  10.3 us
    pallas_call x1, Pallas kernels, legendre_sums(): pl.pallas_call(legendre_kernel, name='legendre', grid=(STEPS,), in_specs=...  9.83 us
    pallas_call x1, Pallas kernels, make_grid(): pl.pallas_call(grid_kernel, name='dft', in_specs=[SMEM, ANY, VMEM, ANY],...  7.71 us
    all_to_all x1, waiting for transfers between devices, on_device(): lax.all_to_all(hold(sent, right, left), 'spec', split_axis=0, concat_axis...  6.76 us
    ppermute x3, starting transfers between devices, on_device(): lax.ppermute(boosts, 'member', [(s, (s + o) % MEM) for s in range(MEM)])  5.22 us
    pallas_call x1, Pallas kernels, pack(): pl.pallas_call(pack_kernel, name='pack', in_specs=[SMEM, SMEM, SMEM, SMEM...  3.97 us
  transfers between devices with their start and end apart: 10, of which 3 were waited for; matrix products, arithmetic and copies ran while one was open for 0% of the time, Pallas kernels for 38%

profile of v1, /device:TPU:24, one launch (start us, length us, event | category | flops | bytes accessed | tf_op | source)
XLA Modules:
  0.0 89.9 jit_solution(17897237629855448247)
XLA Ops:
  0.7 4.0 %pack.1 = (s32[64]{0:T(128)S(1)}, bf16[2,152,16,128]{3,2,1,0:T(8,128)(2,1)S(1)}, bf16[152,16,128]{2,1,0:T(8,128)(2,1)S(1)}, bf16[152,16,128]{2,1,0:T(8,128)(2,1)S(1)}) custom-call(s32[8]{0:T(128)} %counts.1, s32[8]{0:T(128)} %dest.1, s32[1280]{0:T(1024)} %assignment.1, s32[2]{0:T(128)S(1)} %pad_add_fusion.place, bf16[2,20,16,1280]{3,2,1,0:T(8,128)(2,1)} %bitcast.28), custom_call_target="tpu_custom_call" | custom-call | bytes 6000000 | tf_op jit(solution)/shard_map/pack/pallas_call | solution.py:131
  4.7 3.9 %collective-permute-start.3 = (bf16[152,16,128]{2,1,0:T(8,128)(2,1)S(1)}, bf16[152,16,128]{2,1,0:T(8,128)(2,1)S(1)}, u32[]{:S(2)}, u32[]{:S(2)}) collective-permute-start(bf16[152,16,128]{2,1,0:T(8,128)(2,1)S(1)} %get-tuple-element.63), channel_id=1, source_target_pairs={{0,64},{64,128},{128,192},{1,65},{65,129},{129,193},{2,66},{66,130... | collective-permute-start | bytes 1867784 | tf_op jit(solution)/shard_map/ppermute | solution.py:506
  8.6 1.3 %collective-permute-start.4 = (bf16[152,16,128]{2,1,0:T(8,128)(2,1)S(1)}, bf16[152,16,128]{2,1,0:T(8,128)(2,1)}, u32[]{:S(2)}, u32[]{:S(2)}) collective-permute-start(bf16[152,16,128]{2,1,0:T(8,128)(2,1)S(1)} %get-tuple-element.64), channel_id=1, source_target_pairs={{64,0},{128,64},{192,128},{65,1},{129,65},{193,129},{66,2},{130,66... | collective-permute-start | bytes 1867784 | tf_op jit(solution)/shard_map/ppermute | solution.py:507
  9.9 9.8 %legendre.2.refs_3_.refs_0_ = bf16[64,48,128]{2,1,0:T(8,128)(2,1)} custom-call(s32[64]{0:T(128)S(1)} %get-tuple-element.61.tab.refs_0_, bf16[2,20,16,1280]{3,2,1,0:T(8,128)(2,1)} %bitcast.29, bf16[20,1280,256]{2,1,0:T(8,128)(2,1)} %legendre.3), custom_call_target="tpu_custom_call" | custom-call | flops 900000000 | bytes 16000000 | tf_op jit(solution)/shard_map/legendre/pallas_call | solution.py:335
  19.7 2.1 %collective-permute-done.3.refs_2_ = bf16[152,16,128]{2,1,0:T(8,128)(2,1)S(1)} collective-permute-done((bf16[152,16,128]{2,1,0:T(8,128)(2,1)S(1)}, bf16[152,16,128]{2,1,0:T(8,128)(2,1)S(1)}, u32[]{:S(2)}, u32[]{:S(2)}) %collective-permute-start.3) | collective-permute-done | bytes 622624 | tf_op jit(solution)/shard_map/ppermute | solution.py:506
  21.8 0.7 relay1r.1.refs_3_.refs_1_
  22.6 5.3 %collective-permute-start.6 = (bf16[152,16,128]{2,1,0:T(8,128)(2,1)S(1)}, bf16[152,16,128]{2,1,0:T(8,128)(2,1)}, u32[]{:S(2)}, u32[]{:S(2)}) collective-permute-start(bf16[152,16,128]{2,1,0:T(8,128)(2,1)S(1)} %relay1r.1.refs_3_.refs_1_), channel_id=1, source_target_pairs={{0,64},{64,128},{128,192},{1,65},{65,129},{129,193},{2,66},{66,130... | collective-permute-start | bytes 1867784 | tf_op jit(solution)/shard_map/ppermute | solution.py:511
  27.9 0.7 relay1l.1.refs_2_.refs_4_
  28.6 1.3 %collective-permute-start.5 = (bf16[152,16,128]{2,1,0:T(8,128)(2,1)S(1)}, bf16[152,16,128]{2,1,0:T(8,128)(2,1)}, u32[]{:S(2)}, u32[]{:S(2)}) collective-permute-start(bf16[152,16,128]{2,1,0:T(8,128)(2,1)S(1)} %relay1l.1.refs_2_.refs_4_), channel_id=1, source_target_pairs={{64,0},{128,64},{192,128},{65,1},{129,65},{193,129},{66,2},{130,66... | collective-permute-start | bytes 1867784 | tf_op jit(solution)/shard_map/ppermute | solution.py:513
  29.9 13.7 %all-to-all-start = ((bf16[64,48,128]{2,1,0:T(8,128)(2,1)}), bf16[64,48,128]{2,1,0:T(8,128)(2,1)}, u32[]{:S(2)}, u32[]{:S(2)}) async-start(bf16[64,48,128]{2,1,0:T(8,128)(2,1)} %hold.1), calls=%async_computation | async-start | bytes 1572864 | tf_op jit(solution)/shard_map/all_to_all | solution.py:514
  43.6 0.7 relay2r.1.refs_4_
  44.3 5.4 %collective-permute-start.10 = (bf16[152,16,128]{2,1,0:T(8,128)(2,1)S(1)}, bf16[152,16,128]{2,1,0:T(8,128)(2,1)}, u32[]{:S(2)}, u32[]{:S(2)}) collective-permute-start(bf16[152,16,128]{2,1,0:T(8,128)(2,1)S(1)} %relay2r.1.refs_4_), channel_id=1, source_target_pairs={{0,64},{64,128},{128,192},{1,65},{65,129},{129,193},{2,66},{66,130... | collective-permute-start | bytes 1867784 | tf_op jit(solution)/shard_map/ppermute | solution.py:517
  49.7 0.7 relay2l.1.after
  50.5 1.3 %collective-permute-start.11 = (bf16[152,16,128]{2,1,0:T(8,128)(2,1)S(1)}, bf16[152,16,128]{2,1,0:T(8,128)(2,1)}, u32[]{:S(2)}, u32[]{:S(2)}) collective-permute-start(bf16[152,16,128]{2,1,0:T(8,128)(2,1)S(1)} %relay2l.1.after), channel_id=1, source_target_pairs={{64,0},{128,64},{192,128},{65,1},{129,65},{193,129},{66,2},{130,66... | collective-permute-start | bytes 1867784 | tf_op jit(solution)/shard_map/ppermute | solution.py:519
  51.8 10.3 %table.1 = (bf16[5,2560,256]{2,1,0:T(8,128)(2,1)}, f32[8,2560]{1,0:T(8,128)S(1)}, s32[1]{0:T(128)}) custom-call(s32[64]{0:T(128)S(1)} %get-tuple-element.61.tab.refs_0_, f32[10,128]{1,0:T(8,128)S(1)} %convert_bitcast_fusion.waves, bf16[152,16,128]{2,1,0:T(8,128)(2,1)S(1)} %relay2l.1.after), custom_call_target="tpu_custom_call" | custom-call | flops 60000002048 | bytes 8000000 | tf_op jit(solution)/shard_map/table/pallas_call | solution.py:421
  62.1 0.6 copy-done
  63.4 6.8 %all-to-all-done.blocks = bf16[64,48,128]{2,1,0:T(8,128)(2,1)} async-done(((bf16[64,48,128]{2,1,0:T(8,128)(2,1)}), bf16[64,48,128]{2,1,0:T(8,128)(2,1)}, u32[]{:S(2)}, u32[]{:S(2)}) %all-to-all-start) | async-done | bytes 786464 | tf_op jit(solution)/shard_map/all_to_all | solution.py:514
  70.2 7.7 %dft.1 = (f32[128,2560]{1,0:T(8,128)}, f32[8,128]{1,0:T(8,128)}) custom-call(s32[1]{0:T(128)} %bitcast.11.south, bf16[64,48,128]{2,1,0:T(8,128)(2,1)} %all-to-all-done.blocks, f32[8,2560]{1,0:T(8,128)} %copy-done, bf16[5,2560,256]{2,1,0:T(8,128)(2,1)} %get-tuple-element.66.table), custom_call_target="tpu_custom_call" | custom-call | flops 60000002048 | bytes 9000000 | tf_op jit(solution)/shard_map/dft/pallas_call | solution.py:478
  77.9 2.7 %collective-permute-start.7 = (f32[8,128]{1,0:T(8,128)}, f32[8,128]{1,0:T(8,128)S(1)}, u32[]{:S(2)}, u32[]{:S(2)}) collective-permute-start(f32[8,128]{1,0:T(8,128)} %get-tuple-element.68), channel_id=1, source_target_pairs={{0,64},{64,128},{128,192},{192,0},{1,65},{65,129},{129,193},{193,1... | collective-permute-start | bytes 12296 | tf_op jit(solution)/shard_map/ppermute | solution.py:528
  81.2 3.3 %conditional.1 = (bf16[2,20,2,8,1280]{4,3,2,1,0:T(8,128)(2,1)}) conditional(s32[]{:T(128)} %bitcast.18, (s32[8]{0:T(128)S(1)}, s32[8]{0:T(128)S(1)}, s32[]{:T(128)}, s32[]{:T(128)}, s32[1280]{0:T(1024)}, /*index=5*/bf16[2,20,16,1280]{3,2,1,0:T(8,128)(2,1)}) %tuple.35, (s32[64]{0:T(128)S(1)}, bf16[2,152,16,128]{3,2,1,0:T(8,128)(2,1)S(1)}, ...), branch_computations={%region_0.4_spmd, %region_4.5_spmd} | conditional | flops 7398923 | bytes 44289352 | solution.py:550
  81.2 3.2 %unpack.1 = bf16[2,20,16,1280]{3,2,1,0:T(8,128)(2,1)} custom-call(s32[64]{0:T(128)S(1)} %get-tuple-element.40.refs_0_, bf16[2,152,16,128]{3,2,1,0:T(8,128)(2,1)S(1)} %get-tuple-element.41.refs_1_, bf16[152,16,128]{2,1,0:T(8,128)(2,1)S(1)} %get-tuple-element.42.refs_2_, bf16[152,16,128]{2,1,0:T(8,128)(2,1)} %get-tuple-element.43.refs_3_, ...), custom_call_target="tpu_custom_call" | custom-call | bytes 3000000 | tf_op jit(solution)/shard_map/cond/branch_1_fun/unpack/pallas_call | solution.py:231
  84.4 2.0 %collective-permute-start.9 = (f32[8,128]{1,0:T(8,128)S(1)}, f32[8,128]{1,0:T(8,128)S(1)}, u32[]{:S(2)}, u32[]{:S(2)}) collective-permute-start(f32[8,128]{1,0:T(8,128)S(1)} %copy-done.4), channel_id=1, source_target_pairs={{0,192},{64,0},{128,64},{192,128},{1,193},{65,1},{129,65},{193,129... | collective-permute-start | bytes 12296 | tf_op jit(solution)/shard_map/ppermute | solution.py:528
  86.4 1.7 %collective-permute-done.9 = f32[8,128]{1,0:T(8,128)S(1)} collective-permute-done((f32[8,128]{1,0:T(8,128)S(1)}, f32[8,128]{1,0:T(8,128)S(1)}, u32[]{:S(2)}, u32[]{:S(2)}) %collective-permute-start.9) | collective-permute-done | bytes 4128 | tf_op jit(solution)/shard_map/ppermute | solution.py:528
  88.7 1.3 %fusion = f32[2]{0:T(128)} fusion(f32[8,128]{1,0:T(8,128)S(1)} %copy-done.4, f32[]{:T(128)} %bitcast.17), kind=kLoop, calls=%fused_computation.26 | loop fusion | flops 4 | bytes 20 | tf_op jit(solution)/shard_map/div | solution.py:529
  (26 shorter events, 1.3 us)
Async XLA Ops:
  4.7 17.1 %collective-permute-start.3 = (bf16[152,16,128]{2,1,0:T(8,128)(2,1)S(1)}, bf16[152,16,128]{2,1,0:T(8,128)(2,1)S(1)}, u32[]{:S(2)}, u32[]{:S(2)}) collective-permute-start(bf16[152,16,128]{2,1,0:T(8,128)(2,1)S(1)} %get-tuple-element.63), channel_id=1, source_target_pairs={{0,64},{64,128},{128,192},{1,65},{65,129},{129,193},{2,66},{66,130... | collective-permute-start | bytes 1867784 | tf_op jit(solution)/shard_map/ppermute | solution.py:506
  8.6 19.3 %collective-permute-start.4 = (bf16[152,16,128]{2,1,0:T(8,128)(2,1)S(1)}, bf16[152,16,128]{2,1,0:T(8,128)(2,1)}, u32[]{:S(2)}, u32[]{:S(2)}) collective-permute-start(bf16[152,16,128]{2,1,0:T(8,128)(2,1)S(1)} %get-tuple-element.64), channel_id=1, source_target_pairs={{64,0},{128,64},{192,128},{65,1},{129,65},{193,129},{66,2},{130,66... | collective-permute-start | bytes 1867784 | tf_op jit(solution)/shard_map/ppermute | solution.py:507
  9.9 9.8 %copy-start.3 = (s32[1280]{0:T(1024)S(1)}, s32[1280]{0:T(1024)}, u32[]{:S(2)}) copy-start(s32[1280]{0:T(1024)} %assignment.1) | copy-start | bytes 15364
  21.8 0.8 copy-start.1
  22.6 21.0 %collective-permute-start.6 = (bf16[152,16,128]{2,1,0:T(8,128)(2,1)S(1)}, bf16[152,16,128]{2,1,0:T(8,128)(2,1)}, u32[]{:S(2)}, u32[]{:S(2)}) collective-permute-start(bf16[152,16,128]{2,1,0:T(8,128)(2,1)S(1)} %relay1r.1.refs_3_.refs_1_), channel_id=1, source_target_pairs={{0,64},{64,128},{128,192},{1,65},{65,129},{129,193},{2,66},{66,130... | collective-permute-start | bytes 1867784 | tf_op jit(solution)/shard_map/ppermute | solution.py:511
  28.6 21.1 %collective-permute-start.5 = (bf16[152,16,128]{2,1,0:T(8,128)(2,1)S(1)}, bf16[152,16,128]{2,1,0:T(8,128)(2,1)}, u32[]{:S(2)}, u32[]{:S(2)}) collective-permute-start(bf16[152,16,128]{2,1,0:T(8,128)(2,1)S(1)} %relay1l.1.refs_2_.refs_4_), channel_id=1, source_target_pairs={{64,0},{128,64},{192,128},{65,1},{129,65},{193,129},{66,2},{130,66... | collective-permute-start | bytes 1867784 | tf_op jit(solution)/shard_map/ppermute | solution.py:513
  29.9 40.2 %all-to-all-start = ((bf16[64,48,128]{2,1,0:T(8,128)(2,1)}), bf16[64,48,128]{2,1,0:T(8,128)(2,1)}, u32[]{:S(2)}, u32[]{:S(2)}) async-start(bf16[64,48,128]{2,1,0:T(8,128)(2,1)} %hold.1), calls=%async_computation | async-start | bytes 1572864 | tf_op jit(solution)/shard_map/all_to_all | solution.py:514
  44.3 36.8 %collective-permute-start.10 = (bf16[152,16,128]{2,1,0:T(8,128)(2,1)S(1)}, bf16[152,16,128]{2,1,0:T(8,128)(2,1)}, u32[]{:S(2)}, u32[]{:S(2)}) collective-permute-start(bf16[152,16,128]{2,1,0:T(8,128)(2,1)S(1)} %relay2r.1.refs_4_), channel_id=1, source_target_pairs={{0,64},{64,128},{128,192},{1,65},{65,129},{129,193},{2,66},{66,130... | collective-permute-start | bytes 1867784 | tf_op jit(solution)/shard_map/ppermute | solution.py:517
  50.5 30.7 %collective-permute-start.11 = (bf16[152,16,128]{2,1,0:T(8,128)(2,1)S(1)}, bf16[152,16,128]{2,1,0:T(8,128)(2,1)}, u32[]{:S(2)}, u32[]{:S(2)}) collective-permute-start(bf16[152,16,128]{2,1,0:T(8,128)(2,1)S(1)} %relay2l.1.after), channel_id=1, source_target_pairs={{64,0},{128,64},{192,128},{65,1},{129,65},{193,129},{66,2},{130,66... | collective-permute-start | bytes 1867784 | tf_op jit(solution)/shard_map/ppermute | solution.py:519
  62.1 0.6 copy-start
  70.1 11.0 %copy-start.2 = (bf16[152,16,128]{2,1,0:T(8,128)(2,1)S(1)}, bf16[152,16,128]{2,1,0:T(8,128)(2,1)}, u32[]{:S(2)}) copy-start(bf16[152,16,128]{2,1,0:T(8,128)(2,1)} %copy-done.1) | copy-start | bytes 1867780
  70.1 11.0 %copy-start.5 = (s32[8]{0:T(128)S(1)}, s32[8]{0:T(128)}, u32[]{:S(2)}) copy-start(s32[8]{0:T(128)} %counts.1) | copy-start | bytes 100
  70.2 11.0 %copy-start.6 = (s32[8]{0:T(128)S(1)}, s32[8]{0:T(128)}, u32[]{:S(2)}) copy-start(s32[8]{0:T(128)} %dest.1) | copy-start | bytes 100
  77.9 8.5 %collective-permute-start.7 = (f32[8,128]{1,0:T(8,128)}, f32[8,128]{1,0:T(8,128)S(1)}, u32[]{:S(2)}, u32[]{:S(2)}) collective-permute-start(f32[8,128]{1,0:T(8,128)} %get-tuple-element.68), channel_id=1, source_target_pairs={{0,64},{64,128},{128,192},{192,0},{1,65},{65,129},{129,193},{193,1... | collective-permute-start | bytes 12296 | tf_op jit(solution)/shard_map/ppermute | solution.py:528
  80.5 5.9 %collective-permute-start.8 = (f32[8,128]{1,0:T(8,128)}, f32[8,128]{1,0:T(8,128)S(1)}, u32[]{:S(2)}, u32[]{:S(2)}) collective-permute-start(f32[8,128]{1,0:T(8,128)} %get-tuple-element.68), channel_id=1, source_target_pairs={{0,128},{64,192},{128,0},{192,64},{1,129},{65,193},{129,1},{193,65... | collective-permute-start | bytes 12296 | tf_op jit(solution)/shard_map/ppermute | solution.py:528
  81.2 3.3 %copy-start.4 = (f32[8,128]{1,0:T(8,128)S(1)}, f32[8,128]{1,0:T(8,128)}, u32[]{:S(2)}) copy-start(f32[8,128]{1,0:T(8,128)} %get-tuple-element.68) | copy-start | bytes 12292
  84.4 3.7 %collective-permute-start.9 = (f32[8,128]{1,0:T(8,128)S(1)}, f32[8,128]{1,0:T(8,128)S(1)}, u32[]{:S(2)}, u32[]{:S(2)}) collective-permute-start(f32[8,128]{1,0:T(8,128)S(1)} %copy-done.4), channel_id=1, source_target_pairs={{0,192},{64,0},{128,64},{192,128},{1,193},{65,1},{129,65},{193,129... | collective-permute-start | bytes 12296 | tf_op jit(solution)/shard_map/ppermute | solution.py:528

commit v2 on v1

--- a/solution.py
+++ b/solution.py
@@ -1,3 +1,4 @@
+import functools
 import math
 
 import jax
@@ -9,8 +10,8 @@
 
 NLON = 2560
 NN = 1280
-HALF = NLON // 2
-TILES = HALF // 256
+QUARTER = NLON // 4
+BLOCK = 512
 ROWS = 20
 SPEC = 64
 MEM = 4
@@ -21,14 +22,15 @@
 DEPTH = SPEC * KEEP
 CHUNKS = NN // 128
 CAP = 152
-ROUNDS = 3
-SLOT = 6
-FINE = 8
+ROUNDS = 4
+SLOT = 2 * ROUNDS
+FINE = 10
+MORE = 11
 OFF = 16
 LEN = 36
 RIGHT = [(0, 1), (1, 2), (2, 3)]
 LEFT = [(1, 0), (2, 1), (3, 2)]
-COSINE = [(-1) ** k * math.pi ** (2 * k) / math.factorial(2 * k) for k in range(10)]
+COSINE = [(-1) ** k * math.pi ** (2 * k) / math.factorial(2 * k) for k in range(9)]
 ANY = pl.BlockSpec(memory_space=pl.ANY)
 SMEM = pl.BlockSpec(memory_space=pltpu.SMEM)
 VMEM = pl.BlockSpec(memory_space=pltpu.VMEM)
@@ -76,6 +78,8 @@
                 moves.append((way, a, b, chosen))
         for way, a, b, chosen in moves:
             table[a, 2 * t + way] = pick(chosen, code[a])
+        if t == ROUNDS - 1:
+            more = functools.reduce(lambda x, y: x | y, [move[3] for move in moves])
         for way, a, b, chosen in moves:
             have[b] = have[b] | chosen
             for p in range(8):
@@ -85,45 +89,52 @@
         fine = jnp.where(need[d] & ~have[d] == 0, fine, 0)
         for s in range(2):
             table[d, SLOT + s] = pick(one << par[2 * d + s], code[d])
-    return fine
+    return fine, more
 
 
 def pack_kernel(counts, dest, assignment, place, spectra, tab, own, right, left, held, packed, par, table, sems):
-    fetch = pltpu.make_async_copy(spectra, held, sems.at[0])
-    fetch.start()
+    fetches = [pltpu.make_async_copy(spectra.at[m], held.at[m], sems.at[m]) for m in range(2)]
+    for fetch in fetches:
+        fetch.start()
     for c in range(MEM):
         for i in range(2 * ROUNDS):
             table[c, i] = 0
-    fine = plan(counts, dest, par, table)
+    fine, more = plan(counts, dest, par, table)
     for i in range(2 * ROUNDS + 2):
         tab[i] = table[place[0], i]
     tab[FINE] = fine
+    tab[MORE] = more
     total = jnp.int32(0)
     for r in range(ROWS):
         length = NN - assignment[place[1] * ROWS + r]
         tab[OFF + r] = jnp.minimum(total, CAP)
         tab[LEN + r] = length
         total = total + ((length + 127) >> 7)
-    fetch.wait()
-
-    def row(r, carry):
-        start = tab[OFF + r]
-        for m in range(2):
+    sends = ((right, tab[0], 2), (left, tab[1], 3))
+    keeps = []
+    for m in range(2):
+        fetches[m].wait()
+
+        def row(r, carry):
+            start = tab[OFF + r]
             for k in range(CHUNKS):
                 packed[m, start + k] = held[m, r, :, k * 128 : (k + 1) * 128]
-        return carry
-
-    lax.fori_loop(0, ROWS, row, 0)
-    copies = [
-        pltpu.make_async_copy(packed.at[tab[0], pl.ds(0, CAP)], right, sems.at[1]),
-        pltpu.make_async_copy(packed.at[tab[1], pl.ds(0, CAP)], left, sems.at[2]),
-        pltpu.make_async_copy(packed.at[0, pl.ds(0, CAP)], own.at[0], sems.at[3]),
-        pltpu.make_async_copy(packed.at[1, pl.ds(0, CAP)], own.at[1], sems.at[4]),
-    ]
-    for copy in copies:
-        copy.start()
-    for copy in copies:
-        copy.wait()
+            return carry
+
+        lax.fori_loop(0, ROWS, row, 0)
+        slab = packed.at[m, pl.ds(0, CAP)]
+        for target, code, sem in sends:
+
+            @pl.when(code == m)
+            def _():
+                pltpu.make_async_copy(slab, target, sems.at[sem]).start()
+
+        keeps.append(pltpu.make_async_copy(slab, own.at[m], sems.at[4 + m]))
+        keeps[m].start()
+    for target, code, sem in sends:
+        pltpu.make_async_copy(packed.at[0, pl.ds(0, CAP)], target, sems.at[sem]).wait()
+    for keep in keeps:
+        keep.wait()
 
 
 def pack(counts, dest, assignment, place, spectra):
@@ -143,20 +154,12 @@
             pltpu.VMEM((2, ROWS, 16, NN), jnp.bfloat16),
             pltpu.VMEM((2, CAP + 16, 16, 128), jnp.bfloat16),
             pltpu.SMEM((8,), jnp.int32),
-            pltpu.SMEM((MEM, 8), jnp.int32),
-            pltpu.SemaphoreType.DMA((5,)),
+            pltpu.SMEM((MEM, 16), jnp.int32),
+            pltpu.SemaphoreType.DMA((6,)),
         ],
         compiler_params=PARAMS,
         cost_estimate=pl.CostEstimate(flops=0, bytes_accessed=6_000_000, transcendentals=0),
     )(counts, dest, assignment, place, spectra)
-
-
-def choose(code, slabs, target, sem):
-    for k, slab in enumerate(slabs):
-
-        @pl.when(code == k)
-        def _():
-            pltpu.make_async_copy(slab, target, sem).start()
 
 
 def relay(t, way, tab, own, arrived, after):
@@ -202,36 +205,44 @@
     )(value, *after)
 
 
-def unpack_kernel(*refs):
-    tab, own, *rest = refs
-    slabs = [own.at[0], own.at[1], *rest[: 2 * ROUNDS]]
-    out, plain, packed, sems = rest[2 * ROUNDS + 1 :]
-    for s in range(2):
-        choose(tab[SLOT + s], slabs, packed.at[s, pl.ds(0, CAP)], sems.at[s])
-    for s in range(2):
-        pltpu.make_async_copy(own.at[0], packed.at[s, pl.ds(0, CAP)], sems.at[s]).wait()
+def unpack(tab, own, arrived, flat, weights):
+    codes = sorted(arrived)
+
+    def kernel(*refs):
+        tab, own = refs[:2]
+        out, plain, packed, sems = refs[-4:]
+        slabs = {0: own.at[0], 1: own.at[1], **dict(zip(codes, refs[2:]))}
+        for s in range(2):
+            for code, slab in slabs.items():
+
+                @pl.when(tab[SLOT + s] == code)
+                def _():
+                    pltpu.make_async_copy(slab, packed.at[s, pl.ds(0, CAP)], sems.at[s]).start()
+
         lane = lax.broadcasted_iota(jnp.int32, (16, 128), 1)
-
-        def row(r, carry):
-            start = tab[OFF + r]
-            length = tab[LEN + r]
-            for k in range(CHUNKS):
-                value = packed[s, start + k]
-                kept = jnp.where(lane + k * 128 < length, value, jnp.zeros_like(value))
-                plain[s, r, :, k * 128 : (k + 1) * 128] = kept
-            return carry
-
-        lax.fori_loop(0, ROWS, row, 0)
-        pltpu.make_async_copy(plain.at[s], out.at[s], sems.at[2 + s]).start()
-    for s in range(2):
-        pltpu.make_async_copy(plain.at[s], out.at[s], sems.at[2 + s]).wait()
-
-
-def unpack(tab, own, arrived, after):
-    return pl.pallas_call(
-        unpack_kernel,
+        for s in range(2):
+            pltpu.make_async_copy(own.at[0], packed.at[s, pl.ds(0, CAP)], sems.at[s]).wait()
+
+            def row(r, carry):
+                start = tab[OFF + r]
+                length = tab[LEN + r]
+                for k in range(CHUNKS):
+                    value = packed[s, start + k]
+                    kept = jnp.where(lane + k * 128 < length, value, jnp.zeros_like(value))
+                    plain[s, r, :, k * 128 : (k + 1) * 128] = kept
+                return carry
+
+            for first in range(0, ROWS, 5):
+                lax.fori_loop(first, first + 5, row, 0)
+                rows = pl.ds(first, 5)
+                pltpu.make_async_copy(plain.at[s, rows], out.at[s, rows], sems.at[2 + s]).start()
+        for s in range(2):
+            pltpu.make_async_copy(plain.at[s], out.at[s], sems.at[2 + s]).wait()
+
+    return pl.pallas_call(
+        kernel,
         name="unpack",
-        in_specs=[SMEM] + [ANY] * (2 + 2 * ROUNDS),
+        in_specs=[SMEM] + [ANY] * (2 + len(codes)) + [SMEM],
         out_specs=ANY,
         out_shape=pltpu.HBM((2, ROWS, 16, NN), jnp.bfloat16),
         scratch_shapes=[
@@ -241,7 +252,7 @@
         ],
         compiler_params=PARAMS,
         cost_estimate=pl.CostEstimate(flops=0, bytes_accessed=3_000_000, transcendentals=0),
-    )(tab, own, *arrived, after)
+    )(tab, own, *[arrived[code] for code in codes], flat, weights)
 
 
 def swap_blocks(x):
@@ -270,10 +281,10 @@
     a = jnp.full((8, 128), wave, jnp.int32).astype(jnp.float32)
     x = lax.broadcasted_iota(jnp.int32, (8, 128), 0) * 128 + lax.broadcasted_iota(jnp.int32, (8, 128), 1)
     phase = a * x.astype(jnp.float32)
-    weight = jnp.where(a == 0.0, 1.0, 2.0) * (1.0 / math.sqrt(512 * (NLON // 4)))
-    weight = jnp.where(x < NLON // 4, weight, 0.0)
+    weight = jnp.where(a == 0.0, 1.0, 2.0) * (1.0 / math.sqrt(512 * (QUARTER)))
+    weight = jnp.where(x < QUARTER, weight, 0.0)
     return [
-        jnp.sum(jnp.sum(v * weight, axis=0, keepdims=True), axis=1, keepdims=True) for v in (cosine(phase), cosine(phase + NLON // 4))
+        jnp.sum(jnp.sum(v * weight, axis=0, keepdims=True), axis=1, keepdims=True) for v in (cosine(phase), cosine(phase + QUARTER))
     ]
 
 
@@ -352,11 +363,9 @@
     )(tab, spectra, legendre)
 
 
-def table_kernel(tab, waves, after, out, sign, fast, counted, held, sems):
+def table_kernel(tab, waves, after, out, sign, branch, counted, held, sems):
     step = pl.program_id(0)
     slot = step & 1
-    own = waves[pl.ds(step, 1), :]
-    high = jnp.floor(own * (1.0 / 64))
     k = lax.broadcasted_iota(jnp.int32, (256, 128), 0)
     n = lax.broadcasted_iota(jnp.int32, (256, 128), 1)
     spread = ((k >> 3) * 4 + (k & 3) == n).astype(jnp.float32).astype(jnp.bfloat16)
@@ -365,77 +374,92 @@
         rows = jnp.broadcast_to(row, (128, 128)).astype(jnp.bfloat16)
         return lax.dot_general(spread, rows, (((1,), (1,)), ((), ())), preferred_element_type=jnp.float32)
 
-    a = 64.0 * column(high) + column(own - 64.0 * high)
-    parity = own - 2.0 * jnp.floor(own * 0.5)
-    signs = jnp.broadcast_to(1.0 - 2.0 * parity, (8, 128)).astype(jnp.bfloat16)
-    sign[...] = lax.dot_general(signs, spread, (((1,), (1,)), ((), ())), preferred_element_type=jnp.float32)
-
     @pl.when(step == 0)
     def _():
         counted[...] = jnp.zeros_like(counted)
 
-    chunks = jnp.floor((NN + 127.0 - own) * (1.0 / 128))
-    place = lax.broadcasted_iota(jnp.int32, (128, 128), 0) + step * 128
-    first = lax.broadcasted_iota(jnp.int32, (128, 128), 1) * ROWS
-    within = ((place >= first) & (place < first + ROWS)).astype(jnp.float32).astype(jnp.bfloat16)
-    counted[...] += jnp.dot(
-        jnp.broadcast_to(chunks, (8, 128)).astype(jnp.bfloat16), within, preferred_element_type=jnp.float32
-    )
-
     def store(at):
-        rows = pl.ds(pl.multiple_of(at * 256, 256), 256)
-        return pltpu.make_async_copy(held.at[at & 1], out.at[:, rows, :], sems.at[at & 1])
+        rows = pl.ds(pl.multiple_of(at * BLOCK, BLOCK), BLOCK)
+        return pltpu.make_async_copy(held.at[at & 1], out.at[rows, :], sems.at[at & 1])
 
     @pl.when(step >= 2)
     def _():
         store(step - 2).wait()
 
-    piece = 64
-    lane = n[:piece].astype(jnp.float32)
-    part = ((k[:piece] >> 2) & 1).astype(jnp.float32) * (NLON // 4)
-    for i in range(0, 256, piece):
-        wave = a[i : i + piece]
+    columns = []
+    for part in range(BLOCK // 256):
+        at = step * (BLOCK // 256) + part
+        own = waves[pl.ds(at, 1), :]
+        high = jnp.floor(own * (1.0 / 64))
+        wave = 64.0 * column(high) + column(own - 64.0 * high)
+        turn = cosine(jnp.broadcast_to(own * 128.0, (8, 128)))[0:1]
+        twice = jnp.zeros((256, 128), jnp.float32)
+        for _ in range(3):
+            piece = turn.astype(jnp.bfloat16).astype(jnp.float32)
+            twice = twice + column(2.0 * piece)
+            turn = turn - piece
+        columns.append((wave, twice))
+        left = own - 4.0 * jnp.floor(own * 0.25)
+        one, two, three = (jnp.where(left == v, 1.0, 0.0) for v in (1.0, 2.0, 3.0))
+        line = lax.broadcasted_iota(jnp.int32, (8, 128), 0)
+        signs = jnp.where(
+            line == 0, 1.0 - 2.0 * (one + three), jnp.where(line == 1, 1.0 - one - 2.0 * two - three, one - three)
+        )
+        turned = lax.dot_general(
+            signs.astype(jnp.bfloat16), spread, (((1,), (1,)), ((), ())), preferred_element_type=jnp.float32
+        )
+        line = lax.broadcasted_iota(jnp.int32, (8, 256), 0)
+        sine = (lax.broadcasted_iota(jnp.int32, (8, 256), 1) >> 2) & 1
+        sign[:, part * 256 : (part + 1) * 256] = jnp.where((line == 2) & (sine == 0), -turned, turned)
+        chunks = jnp.floor((NN + 127.0 - own) * (1.0 / 128))
+        place = lax.broadcasted_iota(jnp.int32, (128, 128), 0) + at * 128
+        first = lax.broadcasted_iota(jnp.int32, (128, 128), 1) * ROWS
+        within = ((place >= first) & (place < first + ROWS)).astype(jnp.float32).astype(jnp.bfloat16)
+        counted[...] += jnp.dot(
+            jnp.broadcast_to(chunks, (8, 128)).astype(jnp.bfloat16), within, preferred_element_type=jnp.float32
+        )
+
+    lane = n[:64].astype(jnp.float32)
+    part = ((k[:64] >> 2) & 1).astype(jnp.float32) * QUARTER
+    for i in range(0, BLOCK, 64):
+        wave, twice = (column[i % 256 : i % 256 + 64] for column in columns[i // 256])
         weight = jnp.where(wave == 0.0, 1.0, 2.0)
-        turn = wave * 128.0
         phase = wave * lane + part
         now = cosine(phase) * weight
-        later = cosine(phase + turn) * weight
-        twice = 2.0 * cosine(turn)
-        for j in range(HALF // 128):
-            at = (j % 2) * 128
-            held[slot, j // 2, i : i + piece, at : at + 128] = now.astype(jnp.bfloat16)
+        later = cosine(phase + wave * 128.0) * weight
+        for j in range(QUARTER // 128):
+            held[slot, i : i + 64, j * 128 : (j + 1) * 128] = now.astype(jnp.bfloat16)
             now, later = later, twice * later - now
 
     store(step).start()
 
-    @pl.when(step == DEPTH // 256 - 1)
+    @pl.when(step == DEPTH // BLOCK - 1)
     def _():
         most = jnp.max(counted[...]).astype(jnp.int32)
-        fast[0] = jnp.where((most <= CAP) & (tab[FINE] == 1), 1, 0)
+        branch[0] = jnp.where((most <= CAP) & (tab[FINE] == 1), jnp.where(tab[MORE] != 0, 2, 1), 0)
         store(step - 1).wait()
         store(step).wait()
 
 
 def make_table(tab, waves, after):
-    block = 256
     return pl.pallas_call(
         table_kernel,
         name="table",
-        grid=(DEPTH // block,),
+        grid=(DEPTH // BLOCK,),
         in_specs=[SMEM, pl.BlockSpec((10, 128), lambda i: (0, 0)), ANY],
         out_specs=[
             ANY,
-            pl.BlockSpec((8, block), lambda i: (0, i)),
+            pl.BlockSpec((8, BLOCK), lambda i: (0, i)),
             SMEM,
         ],
         out_shape=[
-            pltpu.HBM((TILES, DEPTH, 256), jnp.bfloat16),
+            pltpu.HBM((DEPTH, QUARTER), jnp.bfloat16),
             jax.ShapeDtypeStruct((8, DEPTH), jnp.float32),
             jax.ShapeDtypeStruct((1,), jnp.int32),
         ],
         scratch_shapes=[
             pltpu.VMEM((8, 128), jnp.float32),
-            pltpu.VMEM((2, TILES, block, 256), jnp.bfloat16),
+            pltpu.VMEM((2, BLOCK, QUARTER), jnp.bfloat16),
             pltpu.SemaphoreType.DMA((2,)),
         ],
         compiler_params=PARAMS,
@@ -443,35 +467,75 @@
     )(tab, waves, after)
 
 
-def grid_kernel(south, blocks, sign, table, out, boosts, arrived, held, stacked, result, sems):
+def boost_kernel(blocks, out, parts, sem):
+    fetch = pltpu.make_async_copy(blocks.at[:, pl.ds(KEEP, 8), :], parts, sem)
+    fetch.start()
+    fetch.wait()
+    total = jnp.sum(parts[...].astype(jnp.float32), axis=0)
+    values = jnp.exp(total[0:2] + total[2:4] + total[4:6])
+    out[...] = jnp.concatenate([values, values, values[0:1] + values[1:2], jnp.zeros((3, 128))], axis=0)
+
+
+def make_boosts(blocks):
+    return pl.pallas_call(
+        boost_kernel,
+        name="boosts",
+        in_specs=[ANY],
+        out_specs=VMEM,
+        out_shape=jax.ShapeDtypeStruct((8, 128), jnp.float32),
+        scratch_shapes=[pltpu.VMEM((SPEC, 8, 128), jnp.bfloat16), pltpu.SemaphoreType.DMA],
+        compiler_params=PARAMS,
+        cost_estimate=pl.CostEstimate(flops=0, bytes_accessed=200_000, transcendentals=0),
+    )(blocks)
+
+
+def weights_kernel(mine, *refs):
+    out = refs[-1]
+    total = mine[...]
+    for other in refs[:-1]:
+        total = total + other[...]
+    share = mine[...] * 8.0 / jnp.broadcast_to(total[4:5], (8, 128))
+    for i in range(2):
+        out[i] = share[i, 0]
+
+
+def make_weights(mine, others):
+    return pl.pallas_call(
+        weights_kernel,
+        name="weights",
+        in_specs=[VMEM] * (1 + len(others)),
+        out_specs=SMEM,
+        out_shape=jax.ShapeDtypeStruct((2,), jnp.float32),
+        compiler_params=PARAMS,
+    )(mine, *others)
+
+
+def grid_kernel(south, blocks, sign, table, out, arrived, held, stacked, sems):
     first = pltpu.make_async_copy(blocks, arrived, sems.at[0])
+    second = pltpu.make_async_copy(table, held, sems.at[1])
     first.start()
-    tiles = [pltpu.make_async_copy(table.at[j], held.at[j], sems.at[1 + j]) for j in range(TILES)]
-    for tile in tiles:
-        tile.start()
-    first.wait()
-    rows = arrived[...].astype(jnp.float32)[:, :KEEP, :].reshape(DEPTH, 128).astype(jnp.bfloat16)
+    second.start()
     to = lax.broadcasted_iota(jnp.int32, (128, 128), 0)
     by = lax.broadcasted_iota(jnp.int32, (128, 128), 1)
     lat = jnp.where(south[0] == 1, 7 - (to & 7), to & 7)
     order = (by == lat * 16 + (to >> 3)).astype(jnp.float32).astype(jnp.bfloat16)
+    first.wait()
+    rows = arrived[...].astype(jnp.float32)[:, :KEEP, :].reshape(DEPTH, 128).astype(jnp.bfloat16)
     turned = lax.dot_general(order, rows, (((1,), (1,)), ((), ())), preferred_element_type=jnp.float32)
-    stacked[0:128, :] = turned.astype(jnp.bfloat16)
-    stacked[128:256, :] = (turned * sign[0:1, :]).astype(jnp.bfloat16)
-    parts = jnp.sum(arrived[:, KEEP:SENT, :].astype(jnp.float32), axis=0)
-    values = jnp.exp(parts[0:2] + parts[2:4] + parts[4:6])
-    boosts[...] = jnp.concatenate([values, values, values[0:1] + values[1:2], jnp.zeros((3, 128))], axis=0)
-    stores = []
-    for j in range(TILES):
-        tiles[j].wait()
-        got = jnp.dot(stacked[...], held[j], preferred_element_type=jnp.float32)
-        for half in range(2):
-            at = pl.ds(half * HALF + j * 256, 256)
-            result[:, at] = got[half * 128 : half * 128 + 128]
-            stores.append(pltpu.make_async_copy(result.at[:, at], out.at[:, at], sems.at[1 + TILES + 2 * j + half]))
-            stores[-1].start()
-    for store in stores:
-        store.wait()
+    lane = lax.broadcasted_iota(jnp.int32, (128, 128), 1)
+    for k in range(0, DEPTH, 128):
+        x = turned[:, k : k + 128]
+        other = jnp.where((lane & 4) == 0, pltpu.roll(x, 124, 1), pltpu.roll(x, 4, 1))
+        same = x * sign[1:2, k : k + 128]
+        cross = other * sign[2:3, k : k + 128]
+        stacked[0:128, k : k + 128] = x.astype(jnp.bfloat16)
+        stacked[128:256, k : k + 128] = (same + cross).astype(jnp.bfloat16)
+        stacked[256:384, k : k + 128] = (x * sign[0:1, k : k + 128]).astype(jnp.bfloat16)
+        stacked[384:512, k : k + 128] = (same - cross).astype(jnp.bfloat16)
+    second.wait()
+    got = jnp.dot(stacked[...], held[...], preferred_element_type=jnp.float32)
+    for q in range(4):
+        out[:, q * QUARTER : (q + 1) * QUARTER] = got[q * 128 : (q + 1) * 128]
 
 
 def make_grid(south, blocks, sign, table):
@@ -479,17 +543,13 @@
         grid_kernel,
         name="dft",
         in_specs=[SMEM, ANY, VMEM, ANY],
-        out_specs=[ANY, VMEM],
-        out_shape=[
-            pltpu.HBM((128, NLON), jnp.float32),
-            jax.ShapeDtypeStruct((8, 128), jnp.float32),
-        ],
+        out_specs=VMEM,
+        out_shape=pltpu.HBM((128, NLON), jnp.float32),
         scratch_shapes=[
             pltpu.VMEM((SPEC, SENT, 128), jnp.bfloat16),
-            pltpu.VMEM((TILES, DEPTH, 256), jnp.bfloat16),
-            pltpu.VMEM((256, DEPTH), jnp.bfloat16),
-            pltpu.VMEM((128, NLON), jnp.float32),
-            pltpu.SemaphoreType.DMA((1 + 3 * TILES,)),
+            pltpu.VMEM((DEPTH, QUARTER), jnp.bfloat16),
+            pltpu.VMEM((512, DEPTH), jnp.bfloat16),
+            pltpu.SemaphoreType.DMA((2,)),
         ],
         compiler_params=LARGE,
         cost_estimate=pl.CostEstimate(flops=60_000_000_000, bytes_accessed=9_000_000, transcendentals=0),
@@ -503,31 +563,6 @@
 
     place = jnp.stack([member_idx, spec_idx]).astype(jnp.int32)
     tab, own, right, left = pack(clone_counts, destinations, assignment, place, rows)
-    rights = [lax.ppermute(right, "member", RIGHT)]
-    lefts = [lax.ppermute(left, "member", LEFT)]
-    sent = legendre_sums(tab, rows, legendre)
-
-    right = relay(1, 0, tab, own, rights, sent)
-    rights.append(lax.ppermute(right, "member", RIGHT))
-    left = relay(1, 1, tab, own, lefts, right)
-    lefts.append(lax.ppermute(left, "member", LEFT))
-    blocks = lax.all_to_all(hold(sent, right, left), "spec", split_axis=0, concat_axis=0, tiled=True)
-
-    right = relay(2, 0, tab, own, rights, left)
-    rights.append(lax.ppermute(right, "member", RIGHT))
-    left = relay(2, 1, tab, own, lefts, right)
-    lefts.append(lax.ppermute(left, "member", LEFT))
-    arrived = [slab for pair in zip(rights, lefts) for slab in pair]
-
-    table, sign, fast = make_table(tab, assignment.astype(jnp.float32).reshape(10, 128), left)
-    south = (spec_idx >= SPEC // 2).astype(jnp.int32).reshape(1)
-    flat, boosts = make_grid(south, blocks, sign, table)
-    grid = flat.reshape(2, 8, 8, NLON)
-    total = boosts
-    for o in range(1, MEM):
-        total = total + lax.ppermute(boosts, "member", [(s, (s + o) % MEM) for s in range(MEM)])
-    weights = boosts[0:2, 0] * 8.0 / total[4, 0]
-
     def general():
         wave = lax.dynamic_slice_in_dim(assignment, spec_idx * ROWS, ROWS)
         inside = jnp.arange(NN, dtype=jnp.int32)[None, :] < (NN - wave)[:, None]
@@ -547,8 +582,41 @@
                 cloned = jnp.where((mine_now == home * 2 + i)[:, None, None, None], block[i][None], cloned)
         return cloned
 
-    cloned = lax.cond(fast[0] == 1, lambda: unpack(tab, own, arrived, flat), general)
-    return grid, weights, cloned.reshape(2, ROWS, 2, 8, NN)
+    sends = [right, left]
+    seen = [[], []]
+    arrived = {}
+
+    def start(t, way):
+        got = lax.ppermute(sends[way], "member", (RIGHT, LEFT)[way])
+        seen[way].append(got)
+        arrived[2 + 2 * t + way] = got
+
+    for way in range(2):
+        start(0, way)
+    sent = last = legendre_sums(tab, rows, legendre)
+    for t in range(1, ROUNDS - 1):
+        for way in range(2):
+            sends[way] = last = relay(t, way, tab, own, seen[way], last)
+            start(t, way)
+        if t == 1:
+            blocks = lax.all_to_all(hold(sent, *sends), "spec", split_axis=0, concat_axis=0, tiled=True)
+            table, sign, branch = make_table(tab, assignment.astype(jnp.float32).reshape(10, 128), last)
+            last = sign
+    south = (spec_idx >= SPEC // 2).astype(jnp.int32).reshape(1)
+    boosts = make_boosts(blocks)
+    others = [lax.ppermute(boosts, "member", [(s, (s + o) % MEM) for s in range(MEM)]) for o in range(1, MEM)]
+    flat = make_grid(south, blocks, sign, table)
+    weights = make_weights(boosts, others)
+
+    def one_more():
+        slabs = dict(arrived)
+        for way in range(2):
+            last_send = relay(ROUNDS - 1, way, tab, own, seen[way], own)
+            slabs[2 * ROUNDS + way] = lax.ppermute(last_send, "member", (RIGHT, LEFT)[way])
+        return unpack(tab, own, slabs, flat, weights)
+
+    cloned = lax.switch(branch[0], [general, lambda: unpack(tab, own, arrived, flat, weights), one_more])
+    return flat.reshape(2, 8, 8, NLON), weights, cloned.reshape(2, ROWS, 2, 8, NN)
 
 
 def solution(mesh):

time: 90.5 us -> 87.3 us (0.965); the launches traced: 89.9 us -> 85.7 us
  Pallas kernels: 38 us -> 33 us
  starting transfers between devices: 37.3 us -> 40.4 us
  other arithmetic: 1.34 us -> 0.08 us
    pallas_call x2 -> x4, Pallas kernels: 13.6 us -> 10.1 us  [the longest x1 6.36 us: make_table(): pl.pallas_call(table_kernel, name='table', grid=(DEPTH // BLOCK,), in_spe...]
    ppermute x3, starting transfers between devices: 5.22 us -> 8.52 us  [on_device(): lax.ppermute(boosts, 'member', [(s, (s + o) % MEM) for s in range(MEM)])]
    ppermute x3, waiting for transfers between devices: 1.72 us -> 0.01 us  [on_device(): lax.ppermute(boosts, 'member', [(s, (s + o) % MEM) for s in range(MEM)])]
    pallas_call x1, Pallas kernels: 7.71 us -> 6.35 us  [make_grid(): pl.pallas_call(grid_kernel, name='dft', in_specs=[SMEM, ANY, VMEM, ANY],...]
    all_to_all x1, waiting for transfers between devices: 6.76 us -> 8.1 us  [on_device(): lax.all_to_all(hold(sent, *sends), 'spec', split_axis=0, concat_axis=0, t...]
    div x1 -> x0, other arithmetic: 1.25 us -> none  [on_device(): weights = boosts[0:2, 0] * 8.0 / total[4, 0]]
  transfers between devices with their start and end apart: 10 -> 10, of which waited for: 3 -> 2; matrix products, arithmetic and copies ran while one was open for 0% -> 0% of each run, Pallas kernels for 38% -> 31%
where the time goes in v2:
time: 87.3 us; the launch traced here: 85.7 us
  starting transfers between devices  40.4 us (46%)
  Pallas kernels  33 us (38%)
  waiting for transfers between devices  10.2 us (12%)
  between operations  1.53 us (2%)
    ppermute x6, starting transfers between devices, start(): got = lax.ppermute(sends[way], 'member', (RIGHT, LEFT)[way])  18.4 us
    all_to_all x1, starting transfers between devices, on_device(): lax.all_to_all(hold(sent, *sends), 'spec', split_axis=0, concat_axis=0, t...  13.5 us
    pallas_call x1, Pallas kernels, legendre_sums(): pl.pallas_call(legendre_kernel, name='legendre', grid=(STEPS,), in_specs=...  9.83 us
    ppermute x3, starting transfers between devices, on_device(): lax.ppermute(boosts, 'member', [(s, (s + o) % MEM) for s in range(MEM)])  8.52 us
    all_to_all x1, waiting for transfers between devices, on_device(): lax.all_to_all(hold(sent, *sends), 'spec', split_axis=0, concat_axis=0, t...  8.1 us
    pallas_call x1, Pallas kernels, make_table(): pl.pallas_call(table_kernel, name='table', grid=(DEPTH // BLOCK,), in_spe...  6.36 us
    pallas_call x1, Pallas kernels, make_grid(): pl.pallas_call(grid_kernel, name='dft', in_specs=[SMEM, ANY, VMEM, ANY],...  6.35 us
    pallas_call x1, Pallas kernels, pack(): pl.pallas_call(pack_kernel, name='pack', in_specs=[SMEM, SMEM, SMEM, SMEM...  3.73 us
  transfers between devices with their start and end apart: 10, of which 2 were waited for; matrix products, arithmetic and copies ran while one was open for 0% of the time, Pallas kernels for 31%

profile of v2, /device:TPU:24, one launch (start us, length us, event | category | flops | bytes accessed | tf_op | source)
XLA Modules:
  0.0 85.7 jit_solution(17455143872708121861)
XLA Ops:
  0.7 3.7 %pack.1 = (s32[64]{0:T(128)S(1)}, bf16[2,152,16,128]{3,2,1,0:T(8,128)(2,1)S(1)}, bf16[152,16,128]{2,1,0:T(8,128)(2,1)S(1)}, bf16[152,16,128]{2,1,0:T(8,128)(2,1)S(1)}) custom-call(s32[8]{0:T(128)} %counts.1, s32[8]{0:T(128)} %dest.1, s32[1280]{0:T(1024)} %assignment.1, s32[2]{0:T(128)S(1)} %pad_add_fusion.place, bf16[2,20,16,1280]{3,2,1,0:T(8,128)(2,1)} %bitcast.28), custom_call_target="tpu_custom_call" | custom-call | bytes 6000000 | tf_op jit(solution)/shard_map/pack/pallas_call | solution.py:142
  4.5 3.9 %collective-permute-start.5 = (bf16[152,16,128]{2,1,0:T(8,128)(2,1)S(1)}, bf16[152,16,128]{2,1,0:T(8,128)(2,1)S(1)}, u32[]{:S(2)}, u32[]{:S(2)}) collective-permute-start(bf16[152,16,128]{2,1,0:T(8,128)(2,1)S(1)} %get-tuple-element.95), channel_id=1, source_target_pairs={{0,64},{64,128},{128,192},{1,65},{65,129},{129,193},{2,66},{66,130... | collective-permute-start | bytes 1867784 | tf_op jit(solution)/shard_map/ppermute | solution.py:590
  8.3 1.3 %collective-permute-start.6 = (bf16[152,16,128]{2,1,0:T(8,128)(2,1)S(1)}, bf16[152,16,128]{2,1,0:T(8,128)(2,1)}, u32[]{:S(2)}, u32[]{:S(2)}) collective-permute-start(bf16[152,16,128]{2,1,0:T(8,128)(2,1)S(1)} %get-tuple-element.96), channel_id=1, source_target_pairs={{64,0},{128,64},{192,128},{65,1},{129,65},{193,129},{66,2},{130,66... | collective-permute-start | bytes 1867784 | tf_op jit(solution)/shard_map/ppermute | solution.py:590
  9.6 9.8 %legendre.2.refs_3_.refs_0_ = bf16[64,48,128]{2,1,0:T(8,128)(2,1)} custom-call(s32[64]{0:T(128)S(1)} %get-tuple-element.93.tab.refs_0_, bf16[2,20,16,1280]{3,2,1,0:T(8,128)(2,1)} %bitcast.29, bf16[20,1280,256]{2,1,0:T(8,128)(2,1)} %legendre.3), custom_call_target="tpu_custom_call" | custom-call | flops 900000000 | bytes 16000000 | tf_op jit(solution)/shard_map/legendre/pallas_call | solution.py:346
  19.5 2.1 %collective-permute-done.5.refs_2_ = bf16[152,16,128]{2,1,0:T(8,128)(2,1)S(1)} collective-permute-done((bf16[152,16,128]{2,1,0:T(8,128)(2,1)S(1)}, bf16[152,16,128]{2,1,0:T(8,128)(2,1)S(1)}, u32[]{:S(2)}, u32[]{:S(2)}) %collective-permute-start.5) | collective-permute-done | bytes 622624 | tf_op jit(solution)/shard_map/ppermute | solution.py:590
  21.6 0.7 relay1r.1.refs_3_.refs_1_
  22.3 5.2 %collective-permute-start.10 = (bf16[152,16,128]{2,1,0:T(8,128)(2,1)S(1)}, bf16[152,16,128]{2,1,0:T(8,128)(2,1)}, u32[]{:S(2)}, u32[]{:S(2)}) collective-permute-start(bf16[152,16,128]{2,1,0:T(8,128)(2,1)S(1)} %relay1r.1.refs_3_.refs_1_), channel_id=1, source_target_pairs={{0,64},{64,128},{128,192},{1,65},{65,129},{129,193},{2,66},{66,130... | collective-permute-start | bytes 1867784 | tf_op jit(solution)/shard_map/ppermute | solution.py:590
  27.5 0.7 relay1l.1.refs_2_.after
  28.3 1.3 %collective-permute-start.11 = (bf16[152,16,128]{2,1,0:T(8,128)(2,1)S(1)}, bf16[152,16,128]{2,1,0:T(8,128)(2,1)}, u32[]{:S(2)}, u32[]{:S(2)}) collective-permute-start(bf16[152,16,128]{2,1,0:T(8,128)(2,1)S(1)} %relay1l.1.refs_2_.after), channel_id=1, source_target_pairs={{64,0},{128,64},{192,128},{65,1},{129,65},{193,129},{66,2},{130,66... | collective-permute-start | bytes 1867784 | tf_op jit(solution)/shard_map/ppermute | solution.py:590
  29.6 13.5 %all-to-all-start = ((bf16[64,48,128]{2,1,0:T(8,128)(2,1)}), bf16[64,48,128]{2,1,0:T(8,128)(2,1)S(1)}, u32[]{:S(2)}, u32[]{:S(2)}) async-start(bf16[64,48,128]{2,1,0:T(8,128)(2,1)} %hold.1), calls=%async_computation | async-start | bytes 1572864 | tf_op jit(solution)/shard_map/all_to_all | solution.py:602
  43.1 6.4 %table.1 = (bf16[2560,640]{1,0:T(8,128)(2,1)}, f32[8,2560]{1,0:T(8,128)S(1)}, s32[1]{0:T(128)}) custom-call(s32[64]{0:T(128)S(1)} %get-tuple-element.93.tab.refs_0_, f32[10,128]{1,0:T(8,128)S(1)} %convert_bitcast_fusion.waves, bf16[152,16,128]{2,1,0:T(8,128)(2,1)S(1)} %relay1l.1.refs_2_.after), custom_call_target="tpu_custom_call" | custom-call | flops 60000002048 | bytes 8000000 | tf_op jit(solution)/shard_map/table/pallas_call | solution.py:445
  50.1 0.7 relay2r.1.refs_4_
  50.9 5.4 %collective-permute-start.12 = (bf16[152,16,128]{2,1,0:T(8,128)(2,1)S(1)}, bf16[152,16,128]{2,1,0:T(8,128)(2,1)}, u32[]{:S(2)}, u32[]{:S(2)}) collective-permute-start(bf16[152,16,128]{2,1,0:T(8,128)(2,1)S(1)} %relay2r.1.refs_4_), channel_id=1, source_target_pairs={{0,64},{64,128},{128,192},{1,65},{65,129},{129,193},{2,66},{66,130... | collective-permute-start | bytes 1867784 | tf_op jit(solution)/shard_map/ppermute | solution.py:590
  56.3 0.7 relay2l.1
  57.1 1.3 %collective-permute-start.13 = (bf16[152,16,128]{2,1,0:T(8,128)(2,1)S(1)}, bf16[152,16,128]{2,1,0:T(8,128)(2,1)}, u32[]{:S(2)}, u32[]{:S(2)}) collective-permute-start(bf16[152,16,128]{2,1,0:T(8,128)(2,1)S(1)} %relay2l.1), channel_id=1, source_target_pairs={{64,0},{128,64},{192,128},{65,1},{129,65},{193,129},{66,2},{130,66... | collective-permute-start | bytes 1867784 | tf_op jit(solution)/shard_map/ppermute | solution.py:590
  58.4 8.1 %all-to-all-done.blocks = bf16[64,48,128]{2,1,0:T(8,128)(2,1)S(1)} async-done(((bf16[64,48,128]{2,1,0:T(8,128)(2,1)}), bf16[64,48,128]{2,1,0:T(8,128)(2,1)S(1)}, u32[]{:S(2)}, u32[]{:S(2)}) %all-to-all-start) | async-done | bytes 786464 | tf_op jit(solution)/shard_map/all_to_all | solution.py:602
  66.5 0.1 boosts.1.mine
  66.6 6.1 %collective-permute-start.7 = (f32[8,128]{1,0:T(8,128)S(1)}, f32[8,128]{1,0:T(8,128)S(1)}, u32[]{:S(2)}, u32[]{:S(2)}) collective-permute-start(f32[8,128]{1,0:T(8,128)S(1)} %boosts.1.mine), channel_id=1, source_target_pairs={{0,64},{64,128},{128,192},{192,0},{1,65},{65,129},{129,193},{193,1... | collective-permute-start | bytes 12296 | tf_op jit(solution)/shard_map/ppermute | solution.py:607
  72.7 2.5 %collective-permute-start.9 = (f32[8,128]{1,0:T(8,128)S(1)}, f32[8,128]{1,0:T(8,128)S(1)}, u32[]{:S(2)}, u32[]{:S(2)}) collective-permute-start(f32[8,128]{1,0:T(8,128)S(1)} %boosts.1.mine), channel_id=1, source_target_pairs={{0,192},{64,0},{128,64},{192,128},{1,193},{65,1},{129,65},{193,129... | collective-permute-start | bytes 12296 | tf_op jit(solution)/shard_map/ppermute | solution.py:607
  75.1 6.4 %dft.1 = f32[128,2560]{1,0:T(8,128)} custom-call(s32[1]{0:T(128)} %bitcast.12.south, bf16[64,48,128]{2,1,0:T(8,128)(2,1)} %copy-done, f32[8,2560]{1,0:T(8,128)} %copy-done.1, bf16[2560,640]{1,0:T(8,128)(2,1)} %get-tuple-element.98.table), custom_call_target="tpu_custom_call" | custom-call | flops 60000002048 | bytes 9000000 | tf_op jit(solution)/shard_map/dft/pallas_call | solution.py:542
  81.5 0.6 weights.1
  82.2 0.5 copy-done.7
  82.7 3.0 %conditional.1 = (bf16[2,20,2,8,1280]{4,3,2,1,0:T(8,128)(2,1)}) conditional(s32[]{:T(128)} %bitcast.18, (s32[8]{0:T(128)S(1)}, s32[8]{0:T(128)S(1)}, s32[]{:T(128)}, s32[]{:T(128)}, s32[1280]{0:T(1024)}, /*index=5*/bf16[2,20,16,1280]{3,2,1,0:T(8,128)(2,1)}) %tuple.42, (s32[64]{0:T(128)S(1)}, bf16[2,152,16,128]{3,2,1,0:T(8,128)(2,1)S(1)}, ...), branch_computations={%region_0.4_spmd, %region_4.5_spmd, %region_5.6_spmd} | conditional | flops 7398923 | bytes 44289352 | solution.py:618
  82.7 3.0 %unpack.2 = bf16[2,20,16,1280]{3,2,1,0:T(8,128)(2,1)} custom-call(s32[64]{0:T(128)S(1)} %get-tuple-element.63.refs_0_, bf16[2,152,16,128]{3,2,1,0:T(8,128)(2,1)S(1)} %get-tuple-element.64.refs_1_, bf16[152,16,128]{2,1,0:T(8,128)(2,1)} %get-tuple-element.65.refs_2_, bf16[152,16,128]{2,1,0:T(8,128)(2,1)} %get-tuple-element.66.refs_3_, ...), custom_call_target="tpu_custom_call" | custom-call | bytes 3000000 | tf_op jit(solution)/shard_map/cond/branch_1_fun/unpack/pallas_call | solution.py:242
  (27 shorter events, 0.1 us)
Async XLA Ops:
  4.5 17.1 %collective-permute-start.5 = (bf16[152,16,128]{2,1,0:T(8,128)(2,1)S(1)}, bf16[152,16,128]{2,1,0:T(8,128)(2,1)S(1)}, u32[]{:S(2)}, u32[]{:S(2)}) collective-permute-start(bf16[152,16,128]{2,1,0:T(8,128)(2,1)S(1)} %get-tuple-element.95), channel_id=1, source_target_pairs={{0,64},{64,128},{128,192},{1,65},{65,129},{129,193},{2,66},{66,130... | collective-permute-start | bytes 1867784 | tf_op jit(solution)/shard_map/ppermute | solution.py:590
  8.3 19.2 %collective-permute-start.6 = (bf16[152,16,128]{2,1,0:T(8,128)(2,1)S(1)}, bf16[152,16,128]{2,1,0:T(8,128)(2,1)}, u32[]{:S(2)}, u32[]{:S(2)}) collective-permute-start(bf16[152,16,128]{2,1,0:T(8,128)(2,1)S(1)} %get-tuple-element.96), channel_id=1, source_target_pairs={{64,0},{128,64},{192,128},{65,1},{129,65},{193,129},{66,2},{130,66... | collective-permute-start | bytes 1867784 | tf_op jit(solution)/shard_map/ppermute | solution.py:590
  9.6 9.8 %copy-start.6 = (s32[1280]{0:T(1024)S(1)}, s32[1280]{0:T(1024)}, u32[]{:S(2)}) copy-start(s32[1280]{0:T(1024)} %assignment.1) | copy-start | bytes 15364
  21.6 6.0 %copy-start.2 = (bf16[152,16,128]{2,1,0:T(8,128)(2,1)}, bf16[152,16,128]{2,1,0:T(8,128)(2,1)S(1)}, u32[]{:S(2)}) copy-start(bf16[152,16,128]{2,1,0:T(8,128)(2,1)S(1)} %collective-permute-done.5.refs_2_) | copy-start | bytes 1867780
  22.3 27.8 %collective-permute-start.10 = (bf16[152,16,128]{2,1,0:T(8,128)(2,1)S(1)}, bf16[152,16,128]{2,1,0:T(8,128)(2,1)}, u32[]{:S(2)}, u32[]{:S(2)}) collective-permute-start(bf16[152,16,128]{2,1,0:T(8,128)(2,1)S(1)} %relay1r.1.refs_3_.refs_1_), channel_id=1, source_target_pairs={{0,64},{64,128},{128,192},{1,65},{65,129},{129,193},{2,66},{66,130... | collective-permute-start | bytes 1867784 | tf_op jit(solution)/shard_map/ppermute | solution.py:590
  28.3 28.1 %collective-permute-start.11 = (bf16[152,16,128]{2,1,0:T(8,128)(2,1)S(1)}, bf16[152,16,128]{2,1,0:T(8,128)(2,1)}, u32[]{:S(2)}, u32[]{:S(2)}) collective-permute-start(bf16[152,16,128]{2,1,0:T(8,128)(2,1)S(1)} %relay1l.1.refs_2_.after), channel_id=1, source_target_pairs={{64,0},{128,64},{192,128},{65,1},{129,65},{193,129},{66,2},{130,66... | collective-permute-start | bytes 1867784 | tf_op jit(solution)/shard_map/ppermute | solution.py:590
  29.6 36.9 %all-to-all-start = ((bf16[64,48,128]{2,1,0:T(8,128)(2,1)}), bf16[64,48,128]{2,1,0:T(8,128)(2,1)S(1)}, u32[]{:S(2)}, u32[]{:S(2)}) async-start(bf16[64,48,128]{2,1,0:T(8,128)(2,1)} %hold.1), calls=%async_computation | async-start | bytes 1572864 | tf_op jit(solution)/shard_map/all_to_all | solution.py:602
  43.1 7.0 %copy-start.3 = (bf16[152,16,128]{2,1,0:T(8,128)(2,1)S(1)}, bf16[152,16,128]{2,1,0:T(8,128)(2,1)}, u32[]{:S(2)}) copy-start(bf16[152,16,128]{2,1,0:T(8,128)(2,1)} %copy-done.2) | copy-start | bytes 1867780
  49.5 7.6 %copy-start.1 = (f32[8,2560]{1,0:T(8,128)}, f32[8,2560]{1,0:T(8,128)S(1)}, u32[]{:S(2)}) copy-start(f32[8,2560]{1,0:T(8,128)S(1)} %get-tuple-element.97.sign.refs_4_) | copy-start | bytes 245764
  50.9 31.3 %collective-permute-start.12 = (bf16[152,16,128]{2,1,0:T(8,128)(2,1)S(1)}, bf16[152,16,128]{2,1,0:T(8,128)(2,1)}, u32[]{:S(2)}, u32[]{:S(2)}) collective-permute-start(bf16[152,16,128]{2,1,0:T(8,128)(2,1)S(1)} %relay2r.1.refs_4_), channel_id=1, source_target_pairs={{0,64},{64,128},{128,192},{1,65},{65,129},{129,193},{2,66},{66,130... | collective-permute-start | bytes 1867784 | tf_op jit(solution)/shard_map/ppermute | solution.py:590
  57.1 25.1 %collective-permute-start.13 = (bf16[152,16,128]{2,1,0:T(8,128)(2,1)S(1)}, bf16[152,16,128]{2,1,0:T(8,128)(2,1)}, u32[]{:S(2)}, u32[]{:S(2)}) collective-permute-start(bf16[152,16,128]{2,1,0:T(8,128)(2,1)S(1)} %relay2l.1), channel_id=1, source_target_pairs={{64,0},{128,64},{192,128},{65,1},{129,65},{193,129},{66,2},{130,66... | collective-permute-start | bytes 1867784 | tf_op jit(solution)/shard_map/ppermute | solution.py:590
  66.5 8.6 %copy-start = (bf16[64,48,128]{2,1,0:T(8,128)(2,1)}, bf16[64,48,128]{2,1,0:T(8,128)(2,1)S(1)}, u32[]{:S(2)}) copy-start(bf16[64,48,128]{2,1,0:T(8,128)(2,1)S(1)} %all-to-all-done.blocks) | copy-start | bytes 2359300
  66.6 14.9 %collective-permute-start.7 = (f32[8,128]{1,0:T(8,128)S(1)}, f32[8,128]{1,0:T(8,128)S(1)}, u32[]{:S(2)}, u32[]{:S(2)}) collective-permute-start(f32[8,128]{1,0:T(8,128)S(1)} %boosts.1.mine), channel_id=1, source_target_pairs={{0,64},{64,128},{128,192},{192,0},{1,65},{65,129},{129,193},{193,1... | collective-permute-start | bytes 12296 | tf_op jit(solution)/shard_map/ppermute | solution.py:607
  72.7 8.8 %collective-permute-start.8 = (f32[8,128]{1,0:T(8,128)S(1)}, f32[8,128]{1,0:T(8,128)S(1)}, u32[]{:S(2)}, u32[]{:S(2)}) collective-permute-start(f32[8,128]{1,0:T(8,128)S(1)} %boosts.1.mine), channel_id=1, source_target_pairs={{0,128},{64,192},{128,0},{192,64},{1,129},{65,193},{129,1},{193,65... | collective-permute-start | bytes 12296 | tf_op jit(solution)/shard_map/ppermute | solution.py:607
  72.7 8.8 %collective-permute-start.9 = (f32[8,128]{1,0:T(8,128)S(1)}, f32[8,128]{1,0:T(8,128)S(1)}, u32[]{:S(2)}, u32[]{:S(2)}) collective-permute-start(f32[8,128]{1,0:T(8,128)S(1)} %boosts.1.mine), channel_id=1, source_target_pairs={{0,192},{64,0},{128,64},{192,128},{1,193},{65,1},{129,65},{193,129... | collective-permute-start | bytes 12296 | tf_op jit(solution)/shard_map/ppermute | solution.py:607
  75.1 7.1 %copy-start.8 = (s32[8]{0:T(128)S(1)}, s32[8]{0:T(128)}, u32[]{:S(2)}) copy-start(s32[8]{0:T(128)} %counts.1) | copy-start | bytes 100
  75.1 7.1 %copy-start.9 = (s32[8]{0:T(128)S(1)}, s32[8]{0:T(128)}, u32[]{:S(2)}) copy-start(s32[8]{0:T(128)} %dest.1) | copy-start | bytes 100
  82.2 0.5 copy-start.7
